TPU v7x, 32 devices: a whole 2x2x4 slice. The times are simulated.
32 devices in a mesh: dev: 32 (over z, y, x, core).
Axes of the slice: x: 2, y: 2, z: 4, core: 2. Of those that a mesh axis runs over, the one named last changes fastest.
Arguments:
- latents: bfloat16 [256, 256, 384], P('dev'), may hold values from -6 to 6
- cond: bfloat16 [256, 384], P('dev'), may hold values from -6 to 6
- params: bfloat16 [2, 2662400], P(None, 'dev'), may hold values from -2 to 2, as said below
- cotangent: bfloat16 [256, 256, 384], P('dev'), may hold values from -6 to 6
- counts: int32 [32], P('dev'), may hold values from 1 to 8, as said below
Outputs:
- output: bfloat16 [256, 256, 384], P('dev')
- latents_grad: float32 [256, 256, 384], P('dev')
- cond_grad: float32 [256, 384], P('dev')
- param_grads: float32 [2, 2662400], P(None, 'dev')
Inputs may be any that keep to these rules, and one draw needn't show every extreme that they name: Each device holds counts of its 8 slots live, the first ones; the rest are padding. Some device is full and some holds one latent. `params`: block i's parameters in the stated order, zeros from 2659584 on.
All inputs are finite; a program needn't handle non-finite values.
Results may differ from a plain program's by a relative error of at most 0.025.
The roundings to bfloat16 on the way count: a program that leaves them out, or rounds other values in their place, can miss the bound.
Values may be sent and summed in bfloat16 or wider, within the bound.
A program may use at most 192 MiB of HBM per device.

v0:
```python
import math

import jax
import jax.numpy as jnp
from jax import lax
from jax.sharding import PartitionSpec as P

D = 384
H = 6
HD = 64
MLP = 1536
LAYERS = 2


epsilon = 1e-06


def piece_layout():
    return [
        (D, 6 * D),
        (6 * D,),
        (D, 3 * D),
        (D,),
        (D,),
        (D, D),
        (D,),
        (D, MLP),
        (MLP,),
        (MLP, D),
        (D,),
    ]


def unpack(flat_row):
    pieces = []
    offset = 0
    for shape in piece_layout():
        size_now = math.prod(shape)
        pieces.append(flat_row[offset : offset + size_now].reshape(shape))
        offset += size_now
    return pieces


def normalize(values):
    centered = values - jnp.mean(values, axis=-1, keepdims=True)
    inv_std = lax.rsqrt(jnp.mean(centered * centered, axis=-1, keepdims=True) + epsilon)
    return (centered * inv_std, inv_std)


def norm_back(grad_normed, normed, inv_std):
    mean_grad = jnp.mean(grad_normed, axis=-1, keepdims=True)
    mean_cross = jnp.mean(grad_normed * normed, axis=-1, keepdims=True)
    return inv_std * (grad_normed - mean_grad - normed * mean_cross)


def gelu_tanh(values):
    return jax.nn.gelu(values, approximate=True)


def layer_forward(weights, hidden_in, activ):
    w_ada, b_ada, w_qkv, b_query, b_value, w_out, b_out, w_up, b_up, w_down, b_down = weights
    latent_count, seq_len = (hidden_in.shape[0], hidden_in.shape[1])
    row_count = latent_count * seq_len
    modulation = jnp.dot(activ, w_ada, preferred_element_type=jnp.float32) + b_ada.astype(
        jnp.float32
    )
    mods = [piece[:, None, :] for piece in jnp.split(modulation, 6, axis=-1)]
    shift_a, scale_a, gate_a, shift_b, scale_b, gate_b = mods
    normed_x, inv_a = normalize(hidden_in)
    normed_a = (normed_x * (1.0 + scale_a) + shift_a).astype(jnp.bfloat16)
    qkv_bias = jnp.concatenate([b_query, jnp.zeros_like(b_query), b_value]).astype(jnp.float32)
    qkv_all = (
        jnp.dot(normed_a.reshape(row_count, D), w_qkv, preferred_element_type=jnp.float32)
        + qkv_bias
    )
    qkv_all = qkv_all.astype(jnp.bfloat16).reshape(latent_count, seq_len, 3, H, HD)
    queries, key_part, value_part = (qkv_all[:, :, 0], qkv_all[:, :, 1], qkv_all[:, :, 2])
    scores = jnp.einsum(
        "bqhd,bkhd->bhqk", queries, key_part, preferred_element_type=jnp.float32
    ) * HD ** (-0.5)
    log_total = jax.nn.logsumexp(scores, axis=-1, keepdims=True)
    soft_weights = jnp.exp(scores - log_total)
    soft_low = soft_weights.astype(jnp.bfloat16)
    context = jnp.einsum(
        "bhqk,bkhd->bqhd", soft_low, value_part, preferred_element_type=jnp.float32
    )
    context = context.astype(jnp.bfloat16).reshape(row_count, D)
    attended = jnp.dot(context, w_out, preferred_element_type=jnp.float32) + b_out.astype(
        jnp.float32
    )
    attended = attended.reshape(latent_count, seq_len, D)
    middle = hidden_in + gate_a * attended
    normed_mid, inv_b = normalize(middle)
    normed_b = (normed_mid * (1.0 + scale_b) + shift_b).astype(jnp.bfloat16).reshape(row_count, D)
    pre_act = jnp.dot(normed_b, w_up, preferred_element_type=jnp.float32) + b_up.astype(jnp.float32)
    activated = gelu_tanh(pre_act).astype(jnp.bfloat16)
    branch = jnp.dot(activated, w_down, preferred_element_type=jnp.float32) + b_down.astype(
        jnp.float32
    )
    branch = branch.reshape(latent_count, seq_len, D)
    result = middle + gate_b * branch
    saved = (
        mods,
        normed_x,
        inv_a,
        normed_a,
        queries,
        key_part,
        value_part,
        soft_weights,
        soft_low,
        context,
        attended,
        normed_mid,
        inv_b,
        normed_b,
        pre_act,
        activated,
        branch,
    )
    return (result, saved)


def layer_backward(weights, hidden_in, activ, grad_out):
    w_ada, b_ada, w_qkv, b_query, b_value, w_out, b_out, w_up, b_up, w_down, b_down = weights
    latent_count, seq_len = (hidden_in.shape[0], hidden_in.shape[1])
    row_count = latent_count * seq_len
    result, saved = layer_forward(weights, hidden_in, activ)
    (
        mods,
        normed_x,
        inv_a,
        normed_a,
        queries,
        key_part,
        value_part,
        soft_weights,
        soft_low,
        context,
        attended,
        normed_mid,
        inv_b,
        normed_b,
        pre_act,
        activated,
        branch,
    ) = saved
    shift_a, scale_a, gate_a, shift_b, scale_b, gate_b = mods
    grad_branch = (gate_b * grad_out).astype(jnp.bfloat16).reshape(row_count, D)
    grad_gate_b = jnp.sum(grad_out * branch, axis=1)
    grad_w_down = jnp.einsum(
        "rm,rd->md", activated, grad_branch, preferred_element_type=jnp.float32
    )
    grad_b_down = jnp.sum(grad_branch, axis=0, dtype=jnp.float32)
    grad_act = jnp.einsum("rd,md->rm", grad_branch, w_down, preferred_element_type=jnp.float32)
    _, gelu_pull = jax.vjp(gelu_tanh, pre_act)
    grad_pre = gelu_pull(grad_act)[0].astype(jnp.bfloat16)
    grad_w_up = jnp.einsum("rd,rm->dm", normed_b, grad_pre, preferred_element_type=jnp.float32)
    grad_b_up = jnp.sum(grad_pre, axis=0, dtype=jnp.float32)
    grad_norm_b = jnp.einsum("rm,dm->rd", grad_pre, w_up, preferred_element_type=jnp.float32)
    grad_norm_b = grad_norm_b.reshape(latent_count, seq_len, D)
    grad_scale_b = jnp.sum(grad_norm_b * normed_mid, axis=1)
    grad_shift_b = jnp.sum(grad_norm_b, axis=1)
    grad_mid = grad_out + norm_back(grad_norm_b * (1.0 + scale_b), normed_mid, inv_b)
    grad_gate_a = jnp.sum(grad_mid * attended, axis=1)
    grad_attended = (gate_a * grad_mid).astype(jnp.bfloat16).reshape(row_count, D)
    grad_w_out = jnp.einsum("rd,re->de", context, grad_attended, preferred_element_type=jnp.float32)
    grad_b_out = jnp.sum(grad_attended, axis=0, dtype=jnp.float32)
    grad_context = jnp.einsum("re,de->rd", grad_attended, w_out, preferred_element_type=jnp.float32)
    grad_context = grad_context.astype(jnp.bfloat16).reshape(latent_count, seq_len, H, HD)
    grad_soft = jnp.einsum(
        "bqhd,bkhd->bhqk", grad_context, value_part, preferred_element_type=jnp.float32
    )
    grad_value = jnp.einsum(
        "bhqk,bqhd->bkhd", soft_low, grad_context, preferred_element_type=jnp.float32
    )
    row_dot = jnp.sum(grad_soft * soft_weights, axis=-1, keepdims=True)
    grad_scores = (soft_weights * (grad_soft - row_dot)).astype(jnp.bfloat16)
    grad_query = jnp.einsum(
        "bhqk,bkhd->bqhd", grad_scores, key_part, preferred_element_type=jnp.float32
    ) * HD ** (-0.5)
    grad_key = jnp.einsum(
        "bhqk,bqhd->bkhd", grad_scores, queries, preferred_element_type=jnp.float32
    ) * HD ** (-0.5)
    grad_qkv = (
        jnp.stack([grad_query, grad_key, grad_value], axis=2)
        .astype(jnp.bfloat16)
        .reshape(row_count, 3 * D)
    )
    grad_w_qkv = jnp.einsum(
        "rd,re->de", normed_a.reshape(row_count, D), grad_qkv, preferred_element_type=jnp.float32
    )
    grad_b_query = jnp.sum(grad_qkv[:, :D], axis=0, dtype=jnp.float32)
    grad_b_value = jnp.sum(grad_qkv[:, 2 * D :], axis=0, dtype=jnp.float32)
    grad_norm_a = jnp.einsum("re,de->rd", grad_qkv, w_qkv, preferred_element_type=jnp.float32)
    grad_norm_a = grad_norm_a.reshape(latent_count, seq_len, D)
    grad_scale_a = jnp.sum(grad_norm_a * normed_x, axis=1)
    grad_shift_a = jnp.sum(grad_norm_a, axis=1)
    grad_in = grad_mid + norm_back(grad_norm_a * (1.0 + scale_a), normed_x, inv_a)
    grad_modul = jnp.concatenate(
        [grad_shift_a, grad_scale_a, grad_gate_a, grad_shift_b, grad_scale_b, grad_gate_b], axis=-1
    ).astype(jnp.bfloat16)
    grad_w_ada = jnp.einsum("bd,be->de", activ, grad_modul, preferred_element_type=jnp.float32)
    grad_b_ada = jnp.sum(grad_modul, axis=0, dtype=jnp.float32)
    grad_activ = jnp.einsum("be,de->bd", grad_modul, w_ada, preferred_element_type=jnp.float32)
    grad_parts = [
        grad_w_ada,
        grad_b_ada,
        grad_w_qkv,
        grad_b_query,
        grad_b_value,
        grad_w_out,
        grad_b_out,
        grad_w_up,
        grad_b_up,
        grad_w_down,
        grad_b_down,
    ]
    return (grad_in, grad_activ, grad_parts)


def shards(latents, cond, params, cotangent, counts):
    slot_count = latents.shape[0]
    block_count = slot_count // 2
    live_mask = (jnp.arange(slot_count) < counts[0]).astype(jnp.float32)[:, None, None]
    cond_float = cond.astype(jnp.float32)
    activ = jax.nn.silu(cond_float).astype(jnp.bfloat16)

    def blocked(values):
        return values.reshape((block_count, 2) + values.shape[1:])

    def unblocked(values):
        return values.reshape((slot_count,) + values.shape[2:])

    hidden = latents.astype(jnp.float32)
    kept_inputs = []
    kept_weights = []
    for depth in range(LAYERS):
        weights = unpack(lax.all_gather(params[depth], "dev", axis=0, tiled=True))
        kept_inputs.append(hidden)
        kept_weights.append(weights)

        def forward_block(block_item, weights=weights):
            return layer_forward(weights, block_item[0], block_item[1])[0]

        hidden = unblocked(lax.map(forward_block, (blocked(hidden), blocked(activ))))
    output = (hidden * live_mask).astype(jnp.bfloat16)
    grad_hidden = cotangent.astype(jnp.float32) * live_mask
    grad_activ = jnp.zeros(cond_float.shape, jnp.float32)
    padded_len = params.shape[1] * lax.axis_size("dev")
    shard_rows = []
    for depth in reversed(range(LAYERS)):
        weights = unpack(lax.all_gather(params[depth], "dev", axis=0, tiled=True))

        def backward_block(totals, block_item, weights=weights):
            grad_in, grad_act, grad_parts = layer_backward(
                weights, block_item[0], block_item[1], block_item[2]
            )
            return (
                [total + part_now for total, part_now in zip(totals, grad_parts)],
                (grad_in, grad_act),
            )

        start = [jnp.zeros(piece.shape, jnp.float32) for piece in weights]
        totals, (grad_blocks, activ_blocks) = lax.scan(
            backward_block,
            start,
            (blocked(kept_inputs[depth]), blocked(activ), blocked(grad_hidden)),
        )
        grad_hidden = unblocked(grad_blocks)
        grad_activ = grad_activ + unblocked(activ_blocks)
        flat_grad = jnp.concatenate([piece.reshape(-1) for piece in totals])
        flat_grad = jnp.pad(flat_grad, (0, padded_len - flat_grad.shape[0]))
        shard_rows.append(lax.psum_scatter(flat_grad, "dev", scatter_dimension=0, tiled=True))
    param_grads = jnp.stack(shard_rows[::-1])
    _, silu_pull = jax.vjp(jax.nn.silu, cond_float)
    cond_grad = silu_pull(grad_activ)[0]
    return (output, grad_hidden, cond_grad, param_grads)


def solution(mesh):
    return jax.shard_map(
        shards,
        mesh=mesh,
        in_specs=(
            P("dev", None, None),
            P("dev", None),
            P(None, "dev"),
            P("dev", None, None),
            P("dev"),
        ),
        out_specs=(P("dev", None, None), P("dev", None, None), P("dev", None), P(None, "dev")),
        check_vma=False,
    )
```

profile of v0, /device:TPU:0, one launch (start us, length us, event | category | flops | bytes accessed | tf_op | source)
XLA Modules:
  0.0 1599.8 jit_solution(8913930594721595758)
XLA Ops:
  14.7 86.9 %all-gather.5.cloned.1.call-done = bf16[1,2662400]{1,0:T(2,128)(2,1)} async-done(((bf16[1,83200]{1,0:T(2,128)(2,1)}), bf16[1,2662400]{1,0:T(2,128)(2,1)}) %all-gather.5.cloned.1.call-update) | async-done | bytes 5324816 | tf_op jit(solution)/shard_map/all_gather | solution.py:239
  101.6 26.4 %slice_reduce_fusion.4 = (bf16[589824]{0:T(1024)(128)(2,1)S(1)}, bf16[589824]{0:T(1024)(128)(2,1)S(1)}) fusion(bf16[1,2662400]{1,0:T(2,128)(2,1)} %all-gather.5.cloned.1.call-done), kind=kLoop, calls=%fused_computation.395 | loop fusion | bytes 4718592 | tf_op jit(solution)/shard_map/slice | solution.py:39
  131.6 35.4 %slice_reduce_fusion.1 = bf16[884736]{0:T(1024)(128)(2,1)S(1)} fusion(bf16[1,2662400]{1,0:T(2,128)(2,1)} %all-gather.5.cloned.1.call-done), kind=kLoop, calls=%fused_computation.389 | loop fusion | bytes 3538944 | tf_op jit(solution)/shard_map/slice | solution.py:39
  169.3 15.8 slice_reduce_fusion.7
  187.0 5.9 slice_reduce_fusion.9
  197.9 97.6 %while.94 = (s32[]{:T(128)}, f32[4,2,256,384]{3,2,1,0:T(8,128)}, f32[4,2,256,384]{3,2,1,0:T(8,128)}, bf16[4,2,384]{2,1,0:T(2,128)(2,1)S(1)}, bf16[384,2304]{1,0:...) while((s32[]{:T(128)}, f32[4,2,256,384]{3,2,1,0:T(8,128)}, ...), condition=%wide.region_7.8_spmd, body=%wide.region_0.7_spmd.sunk | while | flops 2038266112 | bytes 42192064 | solution.py:246
  205.9 3.7 reshape.1262
  215.9 4.6 convolution_add_fusion.54
  230.1 3.7 reshape.1262
  240.2 4.6 convolution_add_fusion.54
  254.4 3.7 reshape.1262
  264.5 4.6 convolution_add_fusion.54
  278.8 3.7 reshape.1262
  288.8 4.6 convolution_add_fusion.54
  295.6 27.6 %slice_reduce_fusion.2 = (bf16[589824]{0:T(1024)(128)(2,1)S(1)}, bf16[589824]{0:T(1024)(128)(2,1)}) fusion(bf16[1,2662400]{1,0:T(2,128)(2,1)} %all-gather.7.cloned.1.call-done), kind=kLoop, calls=%fused_computation.393 | loop fusion | bytes 4718592 | tf_op jit(solution)/shard_map/slice | solution.py:39
  323.3 3.5 reshape.1169
  328.2 35.4 %slice_reduce_fusion = bf16[884736]{0:T(1024)(128)(2,1)S(1)} fusion(bf16[1,2662400]{1,0:T(2,128)(2,1)} %all-gather.7.cloned.1.call-done), kind=kLoop, calls=%fused_computation.388 | loop fusion | bytes 3538944 | tf_op jit(solution)/shard_map/slice | solution.py:39
  365.9 15.8 slice_reduce_fusion.6
  383.6 5.9 slice_reduce_fusion.8
  394.4 97.7 %while.95 = (s32[]{:T(128)}, f32[4,2,256,384]{3,2,1,0:T(8,128)}, f32[4,2,256,384]{3,2,1,0:T(8,128)}, bf16[4,2,384]{2,1,0:T(2,128)(2,1)S(1)}, bf16[384,2304]{1,0:...) while((s32[]{:T(128)}, f32[4,2,256,384]{3,2,1,0:T(8,128)}, ...), condition=%wide.region_15.16_spmd, body=%wide.region_8.15_spmd.sunk | while | flops 2038266112 | bytes 42192064 | solution.py:246
  402.5 3.7 reshape.1263
  412.5 4.5 convolution_add_fusion.57
  426.8 3.7 reshape.1263
  436.8 4.5 convolution_add_fusion.57
  451.1 3.7 reshape.1263
  461.2 4.5 convolution_add_fusion.57
  475.4 3.7 reshape.1263
  485.5 4.5 convolution_add_fusion.57
  492.1 5.1 convert_multiply_fusion
  499.8 294.2 %while.96 = (s32[]{:T(128)}, f32[384,2304]{1,0:T(8,128)}, f32[2304]{0:T(1024)}, f32[384,1152]{1,0:T(8,128)}, f32[384]{0:T(512)}, /*index=5*/f32[384]{0:T(512)}, ...) while((s32[]{:T(128)}, f32[384,2304]{1,0:T(8,128)}, ...), condition=%wide.region_40.41_spmd.clone, body=%wide.region_16.40_spmd.clone.sunk | while | flops 6125164544 | bytes 324788320 | solution.py:265
  518.2 3.2 convert_reduce_fusion.20
  536.3 3.8 multiply_reduce_fusion.44
  586.0 3.2 convert_reduce_fusion.20
  604.1 3.8 multiply_reduce_fusion.44
  627.0 4.6 convolution_add_fusion.61
  641.8 3.0 fusion.464
  656.0 3.2 convert_reduce_fusion.20
  674.0 3.8 multiply_reduce_fusion.44
  697.0 4.6 convolution_add_fusion.61
  725.9 3.2 convert_reduce_fusion.20
  744.0 3.8 multiply_reduce_fusion.44
  766.9 4.6 convolution_add_fusion.61
  796.6 268.0 %while.97 = (s32[]{:T(128)}, f32[384,2304]{1,0:T(8,128)}, f32[2304]{0:T(1024)}, f32[384,1152]{1,0:T(8,128)}, f32[384]{0:T(512)}, /*index=5*/f32[384]{0:T(512)}, ...) while((s32[]{:T(128)}, f32[384,2304]{1,0:T(8,128)}, ...), condition=%wide.region_65.66_spmd.clone, body=%wide.region_41.65_spmd.clone.sunk | while | flops 6125164544 | bytes 317667264 | solution.py:265
  812.3 3.2 convert_reduce_fusion.24
  830.5 3.7 multiply_reduce_fusion.49
  877.6 3.2 convert_reduce_fusion.24
  895.8 3.7 multiply_reduce_fusion.49
  918.7 4.6 convolution_add_fusion.69
  945.1 3.2 convert_reduce_fusion.24
  963.3 3.7 multiply_reduce_fusion.49
  986.2 4.6 convolution_add_fusion.69
  1012.6 3.2 convert_reduce_fusion.24
  1030.8 3.7 multiply_reduce_fusion.49
  1053.7 4.6 convolution_add_fusion.69
  1074.7 3.2 reshape.1178
  1090.8 16.3 %dynamic-update-slice.25 = f32[2659584]{0:T(1024)} dynamic-update-slice(f32[2659584]{0:T(1024)} %constant_dynamic-update-slice_fusion.24, f32[442368]{0:T(1024)} %reshape.1175, s32[]{} %constant.344) | dynamic-update-slice | bytes 3538948
  1111.9 21.2 %dynamic-update-slice.30 = f32[2659584]{0:T(1024)} dynamic-update-slice(f32[2659584]{0:T(1024)} %constant_dynamic-update-slice_fusion.16, f32[589824]{0:T(1024)} %reshape.1177, s32[]{} %constant.349) | dynamic-update-slice | bytes 4718596
  1134.4 21.0 %dynamic-update-slice.32 = f32[2659584]{0:T(1024)} dynamic-update-slice(f32[2659584]{0:T(1024)} %constant_dynamic-update-slice_fusion.14, f32[589824]{0:T(1024)} %reshape.1178, s32[]{} %constant.351) | dynamic-update-slice | bytes 4718596
  1156.7 9.5 pad.7
  1167.5 16.3 %dynamic-update-slice.14 = f32[2659584]{0:T(1024)} dynamic-update-slice(f32[2659584]{0:T(1024)} %constant_dynamic-update-slice_fusion.25, f32[442368]{0:T(1024)} %reshape.1180, s32[]{} %constant.344) | dynamic-update-slice | bytes 3538948
  1188.6 21.3 %dynamic-update-slice.19 = f32[2659584]{0:T(1024)} dynamic-update-slice(f32[2659584]{0:T(1024)} %constant_dynamic-update-slice_fusion.17, f32[589824]{0:T(1024)} %reshape.1182, s32[]{} %constant.349) | dynamic-update-slice | bytes 4718596
  1211.2 20.0 %dynamic-update-slice.21 = f32[2659584]{0:T(1024)} dynamic-update-slice(f32[2659584]{0:T(1024)} %constant_dynamic-update-slice_fusion.15, f32[589824]{0:T(1024)S(1)} %reshape.1183, s32[]{} %constant.351) | dynamic-update-slice | bytes 4718596
  1232.5 9.4 pad.8
  1243.3 345.5 %all-reduce.7.cloned.1.call-done = (f32[2662400]{0:T(1024)}, f32[2662400]{0:T(1024)}) async-done(((f32[2662400]{0:T(1024)}, f32[2662400]{0:T(1024)}), (f32[2662400]{0:T(1024)}, f32[2662400]{0:T(1024)})) %all-reduce.7.cloned.1.call-update) | async-done | bytes 21299216
  (2471 shorter events, 655.9 us)
Async XLA Ops:
  7.2 94.4 %all-gather.5.cloned.1.call-start = ((), (), s32[]{:S(2)}) async-start(), calls=%async_computation | async-start | bytes 10982400 | tf_op jit(solution)/shard_map/all_gather | solution.py:239
  9.8 285.8 %all-gather.7.cloned.1.call-start = ((), (), s32[]{:S(2)}) async-start(), calls=%async_computation.1 | async-start | bytes 10982400 | tf_op jit(solution)/shard_map/all_gather | solution.py:239
  10.6 1578.2 %all-reduce.7.cloned.1.call-start = ((), (), s32[]{:S(2)}) async-start(), calls=%async_computation.2 | async-start | bytes 42598400
  295.5 27.7 %copy-start.6 = (bf16[384,2304]{1,0:T(8,128)(2,1)}, bf16[384,2304]{1,0:T(8,128)(2,1)S(1)}, u32[]{:S(2)}) copy-start(bf16[384,2304]{1,0:T(8,128)(2,1)S(1)} %get-tuple-element.2484) | copy-start | bytes 5308420
  295.5 27.7 %copy-start.107 = (bf16[2304]{0:T(1024)(128)(2,1)}, bf16[2304]{0:T(1024)(128)(2,1)S(1)}, u32[]{:S(2)}) copy-start(bf16[2304]{0:T(1024)(128)(2,1)S(1)} %get-tuple-element.2600) | copy-start | bytes 13828
  295.5 27.7 %copy-start.120 = (bf16[1536]{0:T(1024)(128)(2,1)}, bf16[1536]{0:T(1024)(128)(2,1)S(1)}, u32[]{:S(2)}) copy-start(bf16[1536]{0:T(1024)(128)(2,1)S(1)} %get-tuple-element.2636) | copy-start | bytes 9220
  295.5 27.7 %copy-start.169 = (bf16[384]{0:T(512)(128)(2,1)}, bf16[384]{0:T(512)(128)(2,1)S(1)}, u32[]{:S(2)}) copy-start(bf16[384]{0:T(512)(128)(2,1)S(1)} %get-tuple-element.2675) | copy-start | bytes 2308
  295.5 27.7 %copy-start.171 = (bf16[384]{0:T(512)(128)(2,1)}, bf16[384]{0:T(512)(128)(2,1)S(1)}, u32[]{:S(2)}) copy-start(bf16[384]{0:T(512)(128)(2,1)S(1)} %get-tuple-element.2676) | copy-start | bytes 2308
  295.6 27.7 %copy-start.178 = (bf16[384]{0:T(512)(128)(2,1)}, bf16[384]{0:T(512)(128)(2,1)S(1)}, u32[]{:S(2)}) copy-start(bf16[384]{0:T(512)(128)(2,1)S(1)} %get-tuple-element.2715) | copy-start | bytes 2308
  295.6 27.7 %copy-start.181 = (bf16[384]{0:T(512)(128)(2,1)}, bf16[384]{0:T(512)(128)(2,1)S(1)}, u32[]{:S(2)}) copy-start(bf16[384]{0:T(512)(128)(2,1)S(1)} %get-tuple-element.2753) | copy-start | bytes 2308
  394.4 97.7 %copy-start.209 = (f32[8]{0:T(128)S(1)}, f32[8]{0:T(128)}, u32[]{:S(2)}) copy-start(f32[8]{0:T(128)} %compare_convert_fusion) | copy-start | bytes 100
  500.0 11.1 copy-start.137
  500.0 11.1 copy-start.184
  500.0 11.1 copy-start.186
  500.0 12.9 copy-start.176
  500.1 15.0 copy-start.123
  503.8 11.0 copy-start.83
  503.8 11.0 copy-start.95
  535.2 7.9 copy-start.16
  567.8 11.1 copy-start.137
  567.8 11.1 copy-start.184
  567.8 11.1 copy-start.186
  567.8 12.9 copy-start.176
  567.8 15.0 copy-start.123
  571.5 11.0 copy-start.83
  571.6 11.0 copy-start.95
  603.0 7.9 copy-start.16
  637.8 11.1 copy-start.137
  637.8 11.1 copy-start.184
  637.8 11.1 copy-start.186
  637.8 12.9 copy-start.176
  637.8 15.0 copy-start.123
  641.5 11.0 copy-start.83
  641.5 11.0 copy-start.95
  673.0 7.9 copy-start.16
  707.7 11.1 copy-start.137
  707.7 11.1 copy-start.184
  707.7 11.1 copy-start.186
  707.8 12.9 copy-start.176
  707.8 15.0 copy-start.123
  711.5 11.0 copy-start.83
  711.5 11.0 copy-start.95
  796.6 8.6 copy-start.139
  799.8 9.1 copy-start.86
  799.8 9.1 copy-start.97
  862.0 8.6 copy-start.139
  865.1 9.1 copy-start.86
  865.1 9.1 copy-start.97
  929.5 8.6 copy-start.139
  932.6 9.1 copy-start.86
  932.6 9.1 copy-start.97
  997.0 8.6 copy-start.139
  1000.1 9.1 copy-start.86
  1000.1 9.1 copy-start.97
  1087.0 20.1 %copy-start.190 = (f32[384]{0:T(512)S(1)}, f32[384]{0:T(512)}, u32[]{:S(2)}) copy-start(f32[384]{0:T(512)} %get-tuple-element.2758) | copy-start | bytes 4612
  1087.0 22.7 %copy-start.93 = (f32[147456]{0:T(1024)S(1)}, f32[147456]{0:T(1024)}, u32[]{:S(2)}) copy-start(f32[147456]{0:T(1024)} %reshape.1176) | copy-start | bytes 1769476
  1107.1 26.0 %copy-start.153 = (f32[1536]{0:T(1024)S(1)}, f32[1536]{0:T(1024)}, u32[]{:S(2)}) copy-start(f32[1536]{0:T(1024)} %get-tuple-element.2763) | copy-start | bytes 18436
  1133.1 22.3 %copy-start.193 = (f32[384]{0:T(512)S(1)}, f32[384]{0:T(512)}, u32[]{:S(2)}) copy-start(f32[384]{0:T(512)} %get-tuple-element.2765) | copy-start | bytes 4612
  1156.7 9.5 copy-start.146
  1166.2 17.6 %copy-start.197 = (f32[384]{0:T(512)S(1)}, f32[384]{0:T(512)}, u32[]{:S(2)}) copy-start(f32[384]{0:T(512)} %get-tuple-element.2557) | copy-start | bytes 4612
  1166.2 18.9 %copy-start.200 = (f32[384]{0:T(512)S(1)}, f32[384]{0:T(512)}, u32[]{:S(2)}) copy-start(f32[384]{0:T(512)} %get-tuple-element.2558) | copy-start | bytes 4612
  1166.2 21.1 %copy-start.201 = (f32[384]{0:T(512)S(1)}, f32[384]{0:T(512)}, u32[]{:S(2)}) copy-start(f32[384]{0:T(512)} %get-tuple-element.2560) | copy-start | bytes 4612
  1183.8 26.1 %copy-start.156 = (f32[1536]{0:T(1024)S(1)}, f32[1536]{0:T(1024)}, u32[]{:S(2)}) copy-start(f32[1536]{0:T(1024)} %get-tuple-element.2562) | copy-start | bytes 18436
  1209.9 21.3 %copy-start.194 = (f32[384]{0:T(512)S(1)}, f32[384]{0:T(512)}, u32[]{:S(2)}) copy-start(f32[384]{0:T(512)} %get-tuple-element.2564) | copy-start | bytes 4612
  (690 other events, 1997.1 us)
Sparse Core Ops, SparseCore 0:
  11.6 89.9 all-gather.4
  104.6 85.8 all-gather.6
  1242.0 346.6 all-reduce.6
where the time goes:
time: 1630 us; the launch traced here: 1600 us
  local copies, waits for them, and re-layouts  622 us (38%)
  waiting for transfers between devices  433 us (27%)
  matrix products  323 us (20%)
  other arithmetic  178 us (11%)
  loops' own time  28.6 us (2%)
    unnamed x4, waiting for transfers between devices  346 us
    slice x14, local copies, waits for them, and re-layouts, unpack(): pieces.append(flat_row[offset:offset + size_now].reshape(shape))  173 us
    unnamed x92, local copies, waits for them, and re-layouts  138 us
    all_gather x2, waiting for transfers between devices, shards(): weights = unpack(lax.all_gather(params[depth], 'dev', axis=0, tiled=True))  86.9 us
    while x1560, local copies, waits for them, and re-layouts  64 us
    dot_general x16, matrix products, layer_forward(): jnp.dot(activated, w_down, preferred_element_type=jnp.float32)  46.3 us
    dot_general x16, matrix products, layer_forward(): jnp.dot(normed_a.reshape(row_count, D), w_qkv, preferred_element_type=jnp...  43.7 us
    dynamic_update_slice x16, other arithmetic, shards(): lax.map(forward_block, (blocked(hidden), blocked(activ)))  38.3 us
  transfers between devices with their start and end apart: 3, of which 2 were waited for; matrix products, arithmetic and copies ran while one was open for 12% of the time, Pallas kernels for 0%

commit v1 on v0

v1 whole, which is shorter than its diff:
```python
import functools

import jax
import jax.numpy as jnp
from jax import lax
from jax.experimental import pallas as pl
from jax.experimental.pallas import tpu as pltpu
from jax.sharding import PartitionSpec as P

D = 384
H = 6
HD = 64
MLP = 1536
SEQ = 256
LAYERS = 2
PAIR = 2
ROWS = PAIR * SEQ
LANES = 128
EPS = 1e-06
GELU_A = 0.7978845608028654
GELU_B = 0.044715
F32 = jnp.float32
BF16 = jnp.bfloat16

R_ADA = 0
R_BADA = 6912
R_QKV = 6930
R_BQ = 10386
R_BV = 10389
R_O = 10392
R_BO = 11544
R_1 = 11547
R_B1 = 16155
R_2 = 16167
R_B2 = 20775
R_END = 20778

VMEM_LIMIT = 62 * 1024 * 1024


def mm(a, b):
    return lax.dot_general(a, b, (((1,), (0,)), ((), ())), preferred_element_type=F32)


def mm_bt(a, b):
    return lax.dot_general(a, b, (((1,), (1,)), ((), ())), preferred_element_type=F32)


def mm_at(a, b):
    return lax.dot_general(a, b, (((0,), (0,)), ((), ())), preferred_element_type=F32)


def slot_of(order, j):
    return sum(((j >> bit) & 1) << place for place, bit in enumerate(order))


def normalize(values):
    centered = values - jnp.mean(values, axis=-1, keepdims=True)
    inv_std = lax.rsqrt(jnp.mean(centered * centered, axis=-1, keepdims=True) + EPS)
    return centered * inv_std, inv_std


def norm_back(grad, normed, inv_std):
    mean_grad = jnp.mean(grad, axis=-1, keepdims=True)
    mean_cross = jnp.mean(grad * normed, axis=-1, keepdims=True)
    return inv_std * (grad - mean_grad - normed * mean_cross)


def per_latent(values):
    return values.reshape(PAIR, SEQ, values.shape[-1])


def flat_rows(values):
    return values.reshape(ROWS, values.shape[-1])


def load_weights(order, chunk, me, half_a, half_b, activ, stage, flat, sem, w):
    n = stage.shape[0]
    first = pltpu.make_async_copy(half_a, stage.at[pl.ds(0, n // 2)], sem.at[0])
    second = pltpu.make_async_copy(half_b, stage.at[pl.ds(n // 2, n // 2)], sem.at[1])
    first.start()
    second.start()
    first.wait()
    second.wait()
    padded = stage.shape[1]

    def spread(owner, carry):
        slot = slot_of(order, owner ^ me)
        flat[pl.ds(owner * chunk, padded), :] = stage[slot].astype(F32)
        return carry

    lax.fori_loop(0, n, spread, 0)

    def matrix(ref, row, depth, width):
        count = width // LANES
        for c in range(count):
            ref[:, c * LANES : (c + 1) * LANES] = flat[
                pl.ds(row + c, depth, stride=count), :
            ].astype(BF16)

    def vector(ref, row, width, start=0):
        for c in range(width // LANES):
            ref[:, start + c * LANES : start + (c + 1) * LANES] = flat[row + c : row + c + 1, :]

    matrix(w["ada"], R_ADA, D, 6 * D)
    matrix(w["qkv"], R_QKV, D, 3 * D)
    matrix(w["o"], R_O, D, D)
    matrix(w["1"], R_1, D, MLP)
    matrix(w["2"], R_2, MLP, D)
    vector(w["bada"], R_BADA, 6 * D)
    w["bqkv"][...] = jnp.zeros((1, 3 * D), F32)
    vector(w["bqkv"], R_BQ, D)
    vector(w["bqkv"], R_BV, D, 2 * D)
    vector(w["bo"], R_BO, D)
    vector(w["b1"], R_B1, MLP)
    vector(w["b2"], R_B2, D)
    modul = mm(activ[...], w["ada"][...]) + w["bada"][...]
    for latent in range(16):
        w["mods"][latent] = modul[latent : latent + 1, :]


WEIGHT_SCRATCH = {
    "ada": ((D, 6 * D), BF16),
    "qkv": ((D, 3 * D), BF16),
    "o": ((D, D), BF16),
    "1": ((D, MLP), BF16),
    "2": ((MLP, D), BF16),
    "bada": ((1, 6 * D), F32),
    "bqkv": ((1, 3 * D), F32),
    "bo": ((1, D), F32),
    "b1": ((1, MLP), F32),
    "b2": ((1, D), F32),
    "mods": ((16, 1, 6 * D), F32),
}
ACT_SCRATCH = {
    "n1": ((ROWS, D), BF16),
    "qkvv": ((ROWS, 3 * D), BF16),
    "ctx": ((ROWS, D), BF16),
    "n2": ((ROWS, D), BF16),
    "act": ((ROWS, MLP), BF16),
    "branch": ((ROWS, D), F32),
}
BACK_SCRATCH = {
    "probs": ((PAIR * H, SEQ, SEQ), BF16),
    "slope": ((ROWS, MLP), BF16),
    "dpre": ((ROWS, MLP), BF16),
    "dbranch": ((ROWS, D), BF16),
    "dctx": ((ROWS, D), BF16),
    "dqkv": ((ROWS, 3 * D), BF16),
    "gqkv": ((D, 3 * D), F32),
    "go": ((D, D), F32),
    "g1": ((D, MLP), F32),
    "g2": ((MLP, D), F32),
    "gbqkv": ((1, 3 * D), F32),
    "gbo": ((1, D), F32),
    "gb1": ((1, MLP), F32),
    "gb2": ((1, D), F32),
    "dmods": ((16, 1, 6 * D), F32),
}


def head_masks():
    lane = lax.broadcasted_iota(jnp.int32, (SEQ, LANES), 1)
    return lane < HD


def split_heads(values, low_half):
    zero = jnp.zeros_like(values)
    return jnp.where(low_half, values, zero), jnp.where(low_half, zero, values)


def forward(step, x, w, s, keep):
    mods = w["mods"][pl.ds(step * PAIR, PAIR)]
    shift_a, scale_a, gate_a, shift_b, scale_b, gate_b = [
        mods[:, :, p * D : (p + 1) * D] for p in range(6)
    ]
    normed_x, inv_a = normalize(x)
    s["n1"][...] = flat_rows(per_latent(normed_x) * (1.0 + scale_a) + shift_a).astype(BF16)
    s["qkvv"][...] = (mm(s["n1"][...], w["qkv"][...]) + w["bqkv"][...]).astype(BF16)

    def attend(index, carry):
        latent = index // (H // 2)
        pair = index % (H // 2)
        rows = pl.ds(pl.multiple_of(latent * SEQ, SEQ), SEQ)
        low_half = head_masks()

        def lanes(part):
            return pl.ds(pl.multiple_of(part * D + pair * LANES, LANES), LANES)

        q_heads = split_heads(s["qkvv"][rows, lanes(0)] * BF16(HD**-0.5), low_half)
        keys = s["qkvv"][rows, lanes(1)]
        v_heads = split_heads(s["qkvv"][rows, lanes(2)], low_half)
        both = []
        for head in range(2):
            scores = mm_bt(q_heads[head], keys)
            top = jnp.max(scores, axis=-1, keepdims=True)
            raised = jnp.exp(scores - top)
            probs = raised * (1.0 / jnp.sum(raised, axis=-1, keepdims=True))
            probs = probs.astype(BF16)
            if keep:
                s["probs"][index * 2 + head] = probs
            both.append(probs)
        context = mm(jnp.concatenate(both, axis=1), jnp.concatenate(v_heads, axis=0))
        s["ctx"][rows, lanes(0)] = context.astype(BF16)
        return carry

    lax.fori_loop(0, PAIR * H // 2, attend, 0)
    attended = mm(s["ctx"][...], w["o"][...]) + w["bo"][...]
    middle = x + flat_rows(gate_a * per_latent(attended))
    normed_mid, inv_b = normalize(middle)
    s["n2"][...] = flat_rows(per_latent(normed_mid) * (1.0 + scale_b) + shift_b).astype(BF16)

    def hidden(index, carry):
        cols = pl.ds(pl.multiple_of(index * D, D), D)
        pre = mm(s["n2"][...], w["1"][:, cols]) + w["b1"][:, cols]
        square = pre * pre
        tanh = jnp.tanh(pre * (GELU_A + GELU_A * GELU_B * square))
        half = 0.5 * (1.0 + tanh)
        s["act"][:, cols] = (pre * half).astype(BF16)
        if keep:
            inner = GELU_A + 3.0 * GELU_A * GELU_B * square
            slope = half + 0.5 * pre * (1.0 - tanh * tanh) * inner
            s["slope"][:, cols] = slope.astype(BF16)
        return carry

    lax.fori_loop(0, MLP // D, hidden, 0)
    branch = mm(s["act"][...], w["2"][...]) + w["b2"][...]
    result = middle + flat_rows(gate_b * per_latent(branch))
    return result, branch, attended, normed_x, inv_a, normed_mid, inv_b, mods


def forward_kernel(order, chunk, names, scalars, half_a, half_b, activ, x_ref, y_ref, stage, flat, sem, *scratch):
    refs = dict(zip(names, scratch))
    step = pl.program_id(0)
    count, me = scalars[0], scalars[1]

    @pl.when(step == 0)
    def _():
        load_weights(order, chunk, me, half_a, half_b, activ, stage, flat, sem, refs)

    @pl.when(step * PAIR < count)
    def _():
        x = flat_rows(x_ref[...].astype(F32))
        y_ref[...] = per_latent(forward(step, x, refs, refs, False)[0])

    @pl.when(step * PAIR >= count)
    def _():
        y_ref[...] = jnp.zeros_like(y_ref)


def backward_step(step, x, grad, w, s, branch, attended, normed_x, inv_a, normed_mid, inv_b, mods):
    shift_a, scale_a, gate_a, shift_b, scale_b, gate_b = [
        mods[:, :, p * D : (p + 1) * D] for p in range(6)
    ]

    def put_mod(piece, values):
        s["dmods"][pl.ds(step * PAIR, PAIR), :, piece * D : (piece + 1) * D] = jnp.sum(
            per_latent(values), axis=1, keepdims=True
        )

    put_mod(5, grad * branch)
    dbranch = flat_rows(gate_b * per_latent(grad)).astype(BF16)
    s["dbranch"][...] = dbranch
    s["gb2"][...] += jnp.sum(dbranch.astype(F32), axis=0, keepdims=True)

    def hidden(index, carry):
        cols = pl.ds(pl.multiple_of(index * D, D), D)
        s["g2"][cols, :] += mm_at(s["act"][:, cols], s["dbranch"][...])
        dact = mm_bt(s["dbranch"][...], w["2"][cols, :])
        dpre = (dact * s["slope"][:, cols].astype(F32)).astype(BF16)
        s["dpre"][:, cols] = dpre
        s["gb1"][:, cols] += jnp.sum(dpre.astype(F32), axis=0, keepdims=True)
        s["g1"][:, cols] += mm_at(s["n2"][...], dpre)
        return carry

    lax.fori_loop(0, MLP // D, hidden, 0)
    dnorm_b = mm_bt(s["dpre"][...], w["1"][...])
    put_mod(4, dnorm_b * normed_mid)
    put_mod(3, dnorm_b)
    grad_mid = grad + norm_back(
        flat_rows(per_latent(dnorm_b) * (1.0 + scale_b)), normed_mid, inv_b
    )
    put_mod(2, grad_mid * attended)
    dattended = flat_rows(gate_a * per_latent(grad_mid)).astype(BF16)
    s["gbo"][...] += jnp.sum(dattended.astype(F32), axis=0, keepdims=True)
    s["go"][...] += mm_at(s["ctx"][...], dattended)
    s["dctx"][...] = mm_bt(dattended, w["o"][...]).astype(BF16)

    def attend(index, carry):
        latent = index // (H // 2)
        pair = index % (H // 2)
        rows = pl.ds(pl.multiple_of(latent * SEQ, SEQ), SEQ)
        low_half = head_masks()

        def lanes(part):
            return pl.ds(pl.multiple_of(part * D + pair * LANES, LANES), LANES)

        q_heads = split_heads(s["qkvv"][rows, lanes(0)] * BF16(HD**-0.5), low_half)
        k_heads = split_heads(s["qkvv"][rows, lanes(1)] * BF16(HD**-0.5), low_half)
        values = s["qkvv"][rows, lanes(2)]
        dctx = s["dctx"][rows, lanes(0)]
        dctx_heads = split_heads(dctx, low_half)
        cross = dctx.astype(F32) * s["ctx"][rows, lanes(0)].astype(F32)
        dscores = []
        for head in range(2):
            own = jnp.where(low_half == (head == 0), cross, 0.0)
            row_dot = jnp.sum(own, axis=-1, keepdims=True)
            dprobs = mm_bt(dctx_heads[head], values)
            probs = s["probs"][index * 2 + head].astype(F32)
            dscores.append((probs * (dprobs - row_dot)).astype(BF16))
        dquery = mm(jnp.concatenate(dscores, axis=1), jnp.concatenate(k_heads, axis=0))
        dkey = mm_at(dscores[0], q_heads[0]) + mm_at(dscores[1], q_heads[1])
        dvalue = mm_at(s["probs"][index * 2], dctx_heads[0]) + mm_at(
            s["probs"][index * 2 + 1], dctx_heads[1]
        )
        s["dqkv"][rows, lanes(0)] = dquery.astype(BF16)
        s["dqkv"][rows, lanes(1)] = dkey.astype(BF16)
        s["dqkv"][rows, lanes(2)] = dvalue.astype(BF16)
        return carry

    lax.fori_loop(0, PAIR * H // 2, attend, 0)
    dqkv = s["dqkv"][...]
    s["gqkv"][...] += mm_at(s["n1"][...], dqkv)
    s["gbqkv"][...] += jnp.sum(dqkv.astype(F32), axis=0, keepdims=True)
    dnorm_a = mm_bt(dqkv, w["qkv"][...])
    put_mod(1, dnorm_a * normed_x)
    put_mod(0, dnorm_a)
    return grad_mid + norm_back(
        flat_rows(per_latent(dnorm_a) * (1.0 + scale_a)), normed_x, inv_a
    )


def pack_grads(order, chunk, me, activ, stage, flat, sem, w, s, out_grads, dactiv_ref):
    n, padded = stage.shape[0], stage.shape[1]

    def matrix(values_of, row, depth, width):
        count = width // LANES
        for c in range(count):
            flat[pl.ds(row + c, depth, stride=count), :] = values_of(c)

    def of_ref(ref):
        return lambda c: ref[:, c * LANES : (c + 1) * LANES]

    def vector(value, row, width, start=0):
        for c in range(width // LANES):
            flat[row + c : row + c + 1, :] = value[:, start + c * LANES : start + (c + 1) * LANES]

    dmods = jnp.concatenate([s["dmods"][latent] for latent in range(16)], axis=0).astype(BF16)
    dmods_wide = dmods.astype(F32)
    dactiv_ref[...] = mm_bt(dmods, w["ada"][...])
    left = activ[...]
    matrix(lambda c: mm_at(left, dmods[:, c * LANES : (c + 1) * LANES]), R_ADA, D, 6 * D)
    vector(jnp.sum(dmods_wide, axis=0, keepdims=True), R_BADA, 6 * D)
    matrix(of_ref(s["gqkv"]), R_QKV, D, 3 * D)
    vector(s["gbqkv"], R_BQ, D)
    vector(s["gbqkv"], R_BV, D, 2 * D)
    matrix(of_ref(s["go"]), R_O, D, D)
    vector(s["gbo"], R_BO, D)
    matrix(of_ref(s["g1"]), R_1, D, MLP)
    vector(s["gb1"], R_B1, MLP)
    matrix(of_ref(s["g2"]), R_2, MLP, D)
    vector(s["gb2"], R_B2, D)
    flat[R_END : flat.shape[0], :] = jnp.zeros((flat.shape[0] - R_END, LANES), F32)

    def gather(owner, carry):
        slot = slot_of(order, owner ^ me)
        stage[slot] = flat[pl.ds(owner * chunk, padded), :].astype(BF16)
        return carry

    lax.fori_loop(0, n, gather, 0)
    copy = pltpu.make_async_copy(stage, out_grads, sem.at[0])
    copy.start()
    copy.wait()


def backward_kernel(order, chunk, names, last, scalars, half_a, half_b, activ, x_ref, g_ref, *rest):
    if last:
        out_ref, *rest = rest
    gin_ref, dactiv_ref, out_grads, stage, flat, sem, *scratch = rest
    refs = dict(zip(names, scratch))
    step = pl.program_id(0)
    count, me = scalars[0], scalars[1]

    @pl.when(step == 0)
    def _():
        load_weights(order, chunk, me, half_a, half_b, activ, stage, flat, sem, refs)
        for name in ("gqkv", "go", "g1", "g2", "gbqkv", "gbo", "gb1", "gb2", "dmods"):
            refs[name][...] = jnp.zeros_like(refs[name])

    @pl.when(step * PAIR < count)
    def _():
        x = flat_rows(x_ref[...].astype(F32))
        result, branch, *kept = forward(step, x, refs, refs, True)
        grad = g_ref[...].astype(F32)
        if last:
            latent = lax.broadcasted_iota(jnp.int32, (PAIR, SEQ, D), 0) + step * PAIR
            live = latent < count
            out_ref[...] = jnp.where(live, per_latent(result), 0.0).astype(BF16)
            grad = jnp.where(live, grad, 0.0)
        gin_ref[...] = per_latent(
            backward_step(step, x, flat_rows(grad), refs, refs, branch, *kept)
        )

    @pl.when(step * PAIR >= count)
    def _():
        gin_ref[...] = jnp.zeros_like(gin_ref)
        if last:
            out_ref[...] = jnp.zeros_like(out_ref)

    @pl.when(step == pl.num_programs(0) - 1)
    def _():
        pack_grads(order, chunk, me, activ, stage, flat, sem, refs, refs, out_grads, dactiv_ref)


def scratch_of(parts):
    names, shapes = [], []
    for part in parts:
        for name, (shape, dtype) in part.items():
            names.append(name)
            shapes.append(pltpu.VMEM(shape, dtype))
    return tuple(names), shapes


def run_forward(order, chunk, scalars, halves, activ, x):
    n, padded = 2 * halves[0].shape[0], halves[0].shape[1]
    names, shapes = scratch_of([WEIGHT_SCRATCH, ACT_SCRATCH])
    block = pl.BlockSpec((PAIR, SEQ, D), lambda i, sc: (i, 0, 0))
    whole = pl.BlockSpec((16, D), lambda i, sc: (0, 0))
    hbm = pl.BlockSpec(memory_space=pl.ANY)
    return pl.pallas_call(
        functools.partial(forward_kernel, order, chunk, names),
        grid_spec=pltpu.PrefetchScalarGridSpec(
            num_scalar_prefetch=1,
            grid=(x.shape[0] // PAIR,),
            in_specs=[hbm, hbm, whole, block],
            out_specs=block,
            scratch_shapes=[
                pltpu.VMEM((n, padded, LANES), BF16),
                pltpu.VMEM(((n - 1) * chunk + padded, LANES), F32),
                pltpu.SemaphoreType.DMA((2,)),
            ]
            + shapes,
        ),
        out_shape=jax.ShapeDtypeStruct(x.shape, F32),
        compiler_params=pltpu.CompilerParams(vmem_limit_bytes=VMEM_LIMIT),
        cost_estimate=pl.CostEstimate(
            flops=8_000_000_000, bytes_accessed=20_000_000, transcendentals=6_000_000
        ),
        name="block_forward",
    )(scalars, *halves, activ, x)


def run_backward(order, chunk, scalars, halves, activ, x, grad, last):
    n, padded = 2 * halves[0].shape[0], halves[0].shape[1]
    names, shapes = scratch_of([WEIGHT_SCRATCH, ACT_SCRATCH, BACK_SCRATCH])
    block = pl.BlockSpec((PAIR, SEQ, D), lambda i, sc: (i, 0, 0))
    whole = pl.BlockSpec((16, D), lambda i, sc: (0, 0))
    hbm = pl.BlockSpec(memory_space=pl.ANY)
    outs = [
        jax.ShapeDtypeStruct(x.shape, F32),
        jax.ShapeDtypeStruct((16, D), F32),
        jax.ShapeDtypeStruct((n, padded, LANES), BF16),
    ]
    out_specs = [block, whole, hbm]
    if last:
        outs = [jax.ShapeDtypeStruct(x.shape, BF16)] + outs
        out_specs = [block] + out_specs
    return pl.pallas_call(
        functools.partial(backward_kernel, order, chunk, names, last),
        grid_spec=pltpu.PrefetchScalarGridSpec(
            num_scalar_prefetch=1,
            grid=(x.shape[0] // PAIR,),
            in_specs=[hbm, hbm, whole, block, block],
            out_specs=out_specs,
            scratch_shapes=[
                pltpu.VMEM((n, padded, LANES), BF16),
                pltpu.VMEM(((n - 1) * chunk + padded, LANES), F32),
                pltpu.SemaphoreType.DMA((2,)),
            ]
            + shapes,
        ),
        out_shape=outs,
        compiler_params=pltpu.CompilerParams(vmem_limit_bytes=VMEM_LIMIT),
        cost_estimate=pl.CostEstimate(
            flops=32_000_000_000, bytes_accessed=40_000_000, transcendentals=6_000_000
        ),
        name="block_backward",
    )(scalars, *halves, activ, x, grad)


def swap(values, bit, n):
    return lax.ppermute(values, "dev", [(i, i ^ (1 << bit)) for i in range(n)])


def gather_halves(order, n, shard):
    held = shard
    for bit in order[:-1]:
        held = jnp.concatenate([held, swap(held, bit, n)], axis=0)
    return held, swap(held, order[-1], n)


def scatter_sum(order, n, parts):
    for bit in order[::-1]:
        half = parts.shape[0] // 2
        sent = swap(parts[half:], bit, n)
        total = parts[:half].astype(F32) + sent.astype(F32)
        parts = total.astype(BF16) if half > 1 else total
    return parts


def shards(latents, cond, params, cotangent, counts):
    n = lax.axis_size("dev")
    chunk = params.shape[1] // LANES
    padded = (chunk + 15) // 16 * 16
    bits = n.bit_length() - 1
    first = list(range(bits - 1, -1, -1))
    second = list(first)
    if bits > 2:
        second[-2], second[-3] = second[-3], second[-2]
    orders = [tuple(first), tuple(second)]
    scalars = jnp.stack([counts[0], lax.axis_index("dev").astype(jnp.int32)])
    cond_float = cond.astype(F32)
    activ = jax.nn.silu(cond_float).astype(BF16)
    activ = jnp.pad(activ, ((0, 16 - activ.shape[0]), (0, 0)))
    rows = params.reshape(LAYERS, chunk, LANES)
    rows = jnp.pad(rows, ((0, 0), (0, padded - chunk), (0, 0)))
    weights = [gather_halves(orders[i], n, rows[i : i + 1]) for i in range(LAYERS)]
    middle = run_forward(orders[0], chunk, scalars, weights[0], activ, latents)
    output, grad_mid, dactiv_2, parts_2 = run_backward(
        orders[1], chunk, scalars, weights[1], activ, middle, cotangent, True
    )
    sum_2 = scatter_sum(orders[1], n, parts_2)
    grad_in, dactiv_1, parts_1 = run_backward(
        orders[0], chunk, scalars, weights[0], activ, latents, grad_mid, False
    )
    sum_1 = scatter_sum(orders[0], n, parts_1)
    param_grads = jnp.concatenate([sum_1, sum_2], axis=0)[:, :chunk].reshape(LAYERS, chunk * LANES)
    _, silu_pull = jax.vjp(jax.nn.silu, cond_float)
    cond_grad = silu_pull((dactiv_1 + dactiv_2)[: cond.shape[0]])[0]
    return (output, grad_in, cond_grad, param_grads)


def solution(mesh):
    return jax.shard_map(
        shards,
        mesh=mesh,
        in_specs=(
            P("dev", None, None),
            P("dev", None),
            P(None, "dev"),
            P("dev", None, None),
            P("dev"),
        ),
        out_specs=(P("dev", None, None), P("dev", None, None), P("dev", None), P(None, "dev")),
        check_vma=False,
    )
```

time: 1630 us -> 407 us (0.25); the launches traced: 1600 us -> 407 us
  local copies, waits for them, and re-layouts: 622 us -> 17.2 us
  matrix products: 323 us -> 0 us
  waiting for transfers between devices: 433 us -> 125 us
  other arithmetic: 178 us -> 6.38 us
  starting transfers between devices: 0.12 us -> 168 us
  Pallas kernels: 0 us -> 88.9 us
  loops' own time: 28.6 us -> 0 us
    unnamed x4 -> x0, waiting for transfers between devices: 346 us -> none
    dot_general x216 -> x0, matrix products: 323 us -> none  [the longest x16 46.3 us: layer_forward(): jnp.dot(activated, w_down, preferred_element_type=jnp.float32)]
    slice x31 -> x11, local copies, waits for them, and re-layouts: 198 us -> 6.78 us  [the longest x10 5.94 us: scatter_sum(): sent = swap(parts[half:], bit, n)]
    ppermute x0 -> x20, starting transfers between devices: none -> 168 us  [swap(): return lax.ppermute(values, 'dev', [(i, i ^ 1 << bit) for i in range(n)])]
    unnamed x92 -> x19, local copies, waits for them, and re-layouts: 138 us -> 5.89 us
    ppermute x0 -> x20, waiting for transfers between devices: none -> 125 us  [swap(): return lax.ppermute(values, 'dev', [(i, i ^ 1 << bit) for i in range(n)])]
    pallas_call x0 -> x3, Pallas kernels: none -> 88.9 us  [the longest x2 71.4 us: run_backward(): pl.pallas_call(functools.partial(backward_kernel, order, chunk, names, la...]
    all_gather x2 -> x0, waiting for transfers between devices: 86.9 us -> none  [shards(): weights = unpack(lax.all_gather(params[depth], 'dev', axis=0, tiled=True))]
  transfers between devices with their start and end apart: 3 -> 20, of which waited for: 2 -> 13; matrix products, arithmetic and copies ran while one was open for 12% -> 4% of each run, Pallas kernels for 0% -> 13%
where the time goes in v1:
time: 407 us
  starting transfers between devices  168 us (41%)
  waiting for transfers between devices  125 us (31%)
  Pallas kernels  88.9 us (22%)
  local copies, waits for them, and re-layouts  17.2 us (4%)
  other arithmetic  6.38 us (2%)
    ppermute x20, starting transfers between devices, swap(): return lax.ppermute(values, 'dev', [(i, i ^ 1 << bit) for i in range(n)])  168 us
    ppermute x20, waiting for transfers between devices, swap(): return lax.ppermute(values, 'dev', [(i, i ^ 1 << bit) for i in range(n)])  125 us
    pallas_call x2, Pallas kernels, run_backward(): pl.pallas_call(functools.partial(backward_kernel, order, chunk, names, la...  71.4 us
    pallas_call x1, Pallas kernels, run_forward(): pl.pallas_call(functools.partial(forward_kernel, order, chunk, names), gr...  17.5 us
  transfers between devices with their start and end apart: 20, of which 13 were waited for; matrix products, arithmetic and copies ran while one was open for 4% of the time, Pallas kernels for 13%

profile of v1, /device:TPU:0, one launch (start us, length us, event | category | flops | bytes accessed | tf_op | source)
XLA Modules:
  0.0 407.0 jit_solution(13096583992439799060)
XLA Ops:
  0.6 1.5 reshape.14
  2.2 0.8 pad_slice_fusion
  3.0 4.0 collective-permute-start.5
  7.1 7.9 %collective-permute-done.5 = bf16[1,656,128]{2,1,0:T(8,128)(2,1)S(1)} collective-permute-done((bf16[1,656,128]{2,1,0:T(8,128)(2,1)S(1)}, bf16[1,656,128]{2,1,0:T(8,128)(2,1)S(1)}, u32[]{:S(2)}, u32[]{:S(2)}) %collective-permute-start.5) | collective-permute-done | bytes 167968 | tf_op jit(solution)/shard_map/ppermute | solution.py:492
  15.0 0.8 collective-permute-start.6
  15.8 3.4 collective-permute-start
  19.1 8.6 %collective-permute-done.6 = bf16[2,656,128]{2,1,0:T(8,128)(2,1)S(1)} collective-permute-done((bf16[2,656,128]{2,1,0:T(8,128)(2,1)S(1)}, bf16[2,656,128]{2,1,0:T(8,128)(2,1)S(1)}, u32[]{:S(2)}, u32[]{:S(2)}) %collective-permute-start.6) | collective-permute-done | bytes 335904 | tf_op jit(solution)/shard_map/ppermute | solution.py:492
  27.7 0.1 pad_maximum_fusion.4
  27.8 1.3 collective-permute-start.7
  29.2 1.7 collective-permute-start.1
  30.9 7.5 %collective-permute-done.1 = bf16[2,656,128]{2,1,0:T(8,128)(2,1)S(1)} collective-permute-done((bf16[2,656,128]{2,1,0:T(8,128)(2,1)S(1)}, bf16[2,656,128]{2,1,0:T(8,128)(2,1)S(1)}, u32[]{:S(2)}, u32[]{:S(2)}) %collective-permute-start.1) | collective-permute-done | bytes 335904 | tf_op jit(solution)/shard_map/ppermute | solution.py:492
  38.5 1.6 collective-permute-start.2
  40.1 3.1 collective-permute-done.7
  43.2 0.1 pad_maximum_fusion.1
  43.3 1.0 collective-permute-start.8
  44.4 12.3 %collective-permute-done.2 = bf16[4,656,128]{2,1,0:T(8,128)(2,1)S(1)} collective-permute-done((bf16[4,656,128]{2,1,0:T(8,128)(2,1)S(1)}, bf16[4,656,128]{2,1,0:T(8,128)(2,1)S(1)}, u32[]{:S(2)}, u32[]{:S(2)}) %collective-permute-start.2) | collective-permute-done | bytes 671776 | tf_op jit(solution)/shard_map/ppermute | solution.py:492
  56.6 0.1 pad_maximum_fusion
  56.7 1.6 collective-permute-start.3
  58.3 0.7 constant_dynamic-update-slice_fusion.8
  59.0 0.7 constant_dynamic-update-slice_fusion.7
  59.8 0.9 constant_dynamic-update-slice_fusion.6
  60.7 22.2 %collective-permute-done.8 = bf16[8,656,128]{2,1,0:T(8,128)(2,1)S(1)} collective-permute-done((bf16[8,656,128]{2,1,0:T(8,128)(2,1)S(1)}, bf16[8,656,128]{2,1,0:T(8,128)(2,1)S(1)}, u32[]{:S(2)}, u32[]{:S(2)}) %collective-permute-start.8) | collective-permute-done | bytes 1343520 | tf_op jit(solution)/shard_map/ppermute | solution.py:492
  82.9 1.2 constant_dynamic-update-slice_fusion.5.half_a
  84.1 0.7 constant_dynamic-update-slice_fusion.3
  84.8 0.8 constant_dynamic-update-slice_fusion.2
  85.5 0.9 constant_dynamic-update-slice_fusion.1
  86.4 1.2 constant_dynamic-update-slice_fusion.half_a
  87.6 0.5 collective-permute-start.4
  88.8 0.6 pad.9.activ
  89.4 0.6 pad_add_fusion.scalars
  90.0 17.5 %block_forward.1.x_ref = f32[8,256,384]{2,1,0:T(8,128)} custom-call(s32[2]{0:T(128)} %pad_add_fusion.scalars, bf16[16,656,128]{2,1,0:T(8,128)(2,1)} %constant_dynamic-update-slice_fusion.5.half_a, bf16[16,656,128]{2,1,0:T(8,128)(2,1)} %collective-permute-done.9.half_b, bf16[16,384]{1,0:T(8,128)(2,1)} %pad.9.activ, bf16[8,256,384]{2,1,0:T(8,128)(2,1)} %x_ref.3), custom_call_target="tpu_custom_call" | custom-call | flops 8000000000 | bytes 20000000 | tf_op jit(solution)/shard_map/block_forward/pallas_call | solution.py:430
  107.5 35.9 %block_backward.2 = (bf16[8,256,384]{2,1,0:T(8,128)(2,1)}, f32[8,256,384]{2,1,0:T(8,128)}, f32[16,384]{1,0:T(8,128)}, bf16[32,656,128]{2,1,0:T(8,128)(2,1)}) custom-call(s32[2]{0:T(128)} %pad_add_fusion.scalars, bf16[16,656,128]{2,1,0:T(8,128)(2,1)} %constant_dynamic-update-slice_fusion.half_a, bf16[16,656,128]{2,1,0:T(8,128)(2,1)} %collective-permute-done.4.half_b, ...), custom_call_target="tpu_custom_call" | custom-call | flops 32000000000 | bytes 40000000 | tf_op jit(solution)/shard_map/block_backward/pallas_call | solution.py:468
  143.4 3.5 slice.86
  146.9 52.5 %collective-permute-start.15 = (bf16[16,656,128]{2,1,0:T(8,128)(2,1)}, bf16[16,656,128]{2,1,0:T(8,128)(2,1)}, u32[]{:S(2)}, u32[]{:S(2)}) collective-permute-start(bf16[16,656,128]{2,1,0:T(8,128)(2,1)} %slice.86), channel_id=1, source_target_pairs={{0,1},{1,0},{2,3},{3,2},{4,5},{5,4},{6,7},{7,6},{8,9},{9,8},{10,11... | collective-permute-start | bytes 8060936 | tf_op jit(solution)/shard_map/ppermute | solution.py:492
  199.4 35.5 %block_backward.3 = (f32[8,256,384]{2,1,0:T(8,128)}, f32[16,384]{1,0:T(8,128)}, bf16[32,656,128]{2,1,0:T(8,128)(2,1)}) custom-call(s32[2]{0:T(128)} %pad_add_fusion.scalars, bf16[16,656,128]{2,1,0:T(8,128)(2,1)} %constant_dynamic-update-slice_fusion.5.half_a, bf16[16,656,128]{2,1,0:T(8,128)(2,1)} %collective-permute-done.9.half_b, ...), custom_call_target="tpu_custom_call" | custom-call | flops 32000000000 | bytes 40000000 | tf_op jit(solution)/shard_map/block_backward/pallas_call | solution.py:468
  234.9 2.1 slice.76
  237.0 38.0 %collective-permute-start.10 = (bf16[16,656,128]{2,1,0:T(8,128)(2,1)S(1)}, bf16[16,656,128]{2,1,0:T(8,128)(2,1)S(1)}, u32[]{:S(2)}, u32[]{:S(2)}) collective-permute-start(bf16[16,656,128]{2,1,0:T(8,128)(2,1)S(1)} %slice.76), channel_id=1, source_target_pairs={{0,1},{1,0},{2,3},{3,2},{4,5},{5,4},{6,7},{7,6},{8,9},{9,8},{10,11... | collective-permute-start | bytes 8060936 | tf_op jit(solution)/shard_map/ppermute | solution.py:492
  274.9 2.6 add_convert_fusion
  277.6 0.1 slice.107
  277.7 49.8 %collective-permute-start.16 = (bf16[8,656,128]{2,1,0:T(8,128)(2,1)S(1)}, bf16[8,656,128]{2,1,0:T(8,128)(2,1)S(1)}, u32[]{:S(2)}, u32[]{:S(2)}) collective-permute-start(bf16[8,656,128]{2,1,0:T(8,128)(2,1)S(1)} %slice.107), channel_id=1, source_target_pairs={{0,4},{1,5},{2,6},{3,7},{4,0},{5,1},{6,2},{7,3},{8,12},{9,13},{10,... | collective-permute-start | bytes 4030472 | tf_op jit(solution)/shard_map/ppermute | solution.py:492
  327.5 0.7 add_convert_fusion.1
  328.2 0.1 slice.99
  328.3 3.3 collective-permute-start.11
  331.6 25.2 %collective-permute-done.16 = bf16[8,656,128]{2,1,0:T(8,128)(2,1)S(1)} collective-permute-done((bf16[8,656,128]{2,1,0:T(8,128)(2,1)S(1)}, bf16[8,656,128]{2,1,0:T(8,128)(2,1)S(1)}, u32[]{:S(2)}, u32[]{:S(2)}) %collective-permute-start.16) | collective-permute-done | bytes 1343520 | tf_op jit(solution)/shard_map/ppermute | solution.py:492
  356.8 0.3 add_convert_fusion.2
  357.2 4.2 %collective-permute-start.17 = (bf16[4,656,128]{2,1,0:T(8,128)(2,1)S(1)}, bf16[4,656,128]{2,1,0:T(8,128)(2,1)S(1)}, u32[]{:S(2)}, u32[]{:S(2)}) collective-permute-start(bf16[4,656,128]{2,1,0:T(8,128)(2,1)S(1)} %slice.109), channel_id=1, source_target_pairs={{0,2},{1,3},{2,0},{3,1},{4,6},{5,7},{6,4},{7,5},{8,10},{9,11},{10,... | collective-permute-start | bytes 2015240 | tf_op jit(solution)/shard_map/ppermute | solution.py:492
  361.3 0.1 collective-permute-done.11
  361.5 0.4 add_convert_fusion.3
  361.9 1.7 collective-permute-start.12
  363.6 12.8 %collective-permute-done.17 = bf16[4,656,128]{2,1,0:T(8,128)(2,1)S(1)} collective-permute-done((bf16[4,656,128]{2,1,0:T(8,128)(2,1)S(1)}, bf16[4,656,128]{2,1,0:T(8,128)(2,1)S(1)}, u32[]{:S(2)}, u32[]{:S(2)}) %collective-permute-start.17) | collective-permute-done | bytes 671776 | tf_op jit(solution)/shard_map/ppermute | solution.py:492
  376.4 0.2 add_convert_fusion.4
  376.6 0.4 collective-permute-start.18
  377.0 1.6 collective-permute-done.12
  378.7 0.2 add_convert_fusion.5
  378.9 0.4 collective-permute-start.13
  379.3 0.6 fusion.6
  380.0 7.5 %collective-permute-done.18 = bf16[2,656,128]{2,1,0:T(8,128)(2,1)S(1)} collective-permute-done((bf16[2,656,128]{2,1,0:T(8,128)(2,1)S(1)}, bf16[2,656,128]{2,1,0:T(8,128)(2,1)S(1)}, u32[]{:S(2)}, u32[]{:S(2)}) %collective-permute-start.18) | collective-permute-done | bytes 335904 | tf_op jit(solution)/shard_map/ppermute | solution.py:492
  387.5 0.1 add_convert_fusion.6
  387.6 1.1 collective-permute-start.19
  388.7 7.8 %collective-permute-done.13 = bf16[2,656,128]{2,1,0:T(8,128)(2,1)S(1)} collective-permute-done((bf16[2,656,128]{2,1,0:T(8,128)(2,1)S(1)}, bf16[2,656,128]{2,1,0:T(8,128)(2,1)S(1)}, u32[]{:S(2)}, u32[]{:S(2)}) %collective-permute-start.13) | collective-permute-done | bytes 335904 | tf_op jit(solution)/shard_map/ppermute | solution.py:492
  396.5 0.1 add_convert_fusion.7
  396.7 1.2 collective-permute-start.14
  397.9 7.8 %collective-permute-done.14 = bf16[1,656,128]{2,1,0:T(8,128)(2,1)S(1)} collective-permute-done((bf16[1,656,128]{2,1,0:T(8,128)(2,1)S(1)}, bf16[1,656,128]{2,1,0:T(8,128)(2,1)S(1)}, u32[]{:S(2)}, u32[]{:S(2)}) %collective-permute-start.14) | collective-permute-done | bytes 167968 | tf_op jit(solution)/shard_map/ppermute | solution.py:492
  405.8 1.2 copy.11
  (34 shorter events, 0.5 us)
Async XLA Ops:
  3.0 11.9 %collective-permute-start.5 = (bf16[1,656,128]{2,1,0:T(8,128)(2,1)S(1)}, bf16[1,656,128]{2,1,0:T(8,128)(2,1)S(1)}, u32[]{:S(2)}, u32[]{:S(2)}) collective-permute-start(bf16[1,656,128]{2,1,0:T(8,128)(2,1)S(1)} %get-tuple-element.18), channel_id=1, source_target_pairs={{0,16},{1,17},{2,18},{3,19},{4,20},{5,21},{6,22},{7,23},{8,24},{9,... | collective-permute-start | bytes 503816 | tf_op jit(solution)/shard_map/ppermute | solution.py:492
  15.0 12.7 %collective-permute-start.6 = (bf16[2,656,128]{2,1,0:T(8,128)(2,1)S(1)}, bf16[2,656,128]{2,1,0:T(8,128)(2,1)S(1)}, u32[]{:S(2)}, u32[]{:S(2)}) collective-permute-start(bf16[2,656,128]{2,1,0:T(8,128)(2,1)S(1)} %pad_maximum_fusion.6), channel_id=1, source_target_pairs={{0,8},{1,9},{2,10},{3,11},{4,12},{5,13},{6,14},{7,15},{8,0},{9,1},... | collective-permute-start | bytes 1007624 | tf_op jit(solution)/shard_map/ppermute | solution.py:492
  15.8 13.4 %collective-permute-start = (bf16[1,656,128]{2,1,0:T(8,128)(2,1)S(1)}, bf16[1,656,128]{2,1,0:T(8,128)(2,1)S(1)}, u32[]{:S(2)}, u32[]{:S(2)}) collective-permute-start(bf16[1,656,128]{2,1,0:T(8,128)(2,1)S(1)} %get-tuple-element.21), channel_id=1, source_target_pairs={{0,16},{1,17},{2,18},{3,19},{4,20},{5,21},{6,22},{7,23},{8,24},{9,... | collective-permute-start | bytes 503816 | tf_op jit(solution)/shard_map/ppermute | solution.py:492
  27.8 15.4 %collective-permute-start.7 = (bf16[4,656,128]{2,1,0:T(8,128)(2,1)S(1)}, bf16[4,656,128]{2,1,0:T(8,128)(2,1)S(1)}, u32[]{:S(2)}, u32[]{:S(2)}) collective-permute-start(bf16[4,656,128]{2,1,0:T(8,128)(2,1)S(1)} %pad_maximum_fusion.4), channel_id=1, source_target_pairs={{0,4},{1,5},{2,6},{3,7},{4,0},{5,1},{6,2},{7,3},{8,12},{9,13},{10,... | collective-permute-start | bytes 2015240 | tf_op jit(solution)/shard_map/ppermute | solution.py:492
  29.2 9.3 %collective-permute-start.1 = (bf16[2,656,128]{2,1,0:T(8,128)(2,1)S(1)}, bf16[2,656,128]{2,1,0:T(8,128)(2,1)S(1)}, u32[]{:S(2)}, u32[]{:S(2)}) collective-permute-start(bf16[2,656,128]{2,1,0:T(8,128)(2,1)S(1)} %pad_maximum_fusion.5), channel_id=1, source_target_pairs={{0,8},{1,9},{2,10},{3,11},{4,12},{5,13},{6,14},{7,15},{8,0},{9,1},... | collective-permute-start | bytes 1007624 | tf_op jit(solution)/shard_map/ppermute | solution.py:492
  38.5 18.1 %collective-permute-start.2 = (bf16[4,656,128]{2,1,0:T(8,128)(2,1)S(1)}, bf16[4,656,128]{2,1,0:T(8,128)(2,1)S(1)}, u32[]{:S(2)}, u32[]{:S(2)}) collective-permute-start(bf16[4,656,128]{2,1,0:T(8,128)(2,1)S(1)} %pad_maximum_fusion.3), channel_id=1, source_target_pairs={{0,2},{1,3},{2,0},{3,1},{4,6},{5,7},{6,4},{7,5},{8,10},{9,11},{10,... | collective-permute-start | bytes 2015240 | tf_op jit(solution)/shard_map/ppermute | solution.py:492
  43.3 39.5 %collective-permute-start.8 = (bf16[8,656,128]{2,1,0:T(8,128)(2,1)S(1)}, bf16[8,656,128]{2,1,0:T(8,128)(2,1)S(1)}, u32[]{:S(2)}, u32[]{:S(2)}) collective-permute-start(bf16[8,656,128]{2,1,0:T(8,128)(2,1)S(1)} %pad_maximum_fusion.1), channel_id=1, source_target_pairs={{0,2},{1,3},{2,0},{3,1},{4,6},{5,7},{6,4},{7,5},{8,10},{9,11},{10,... | collective-permute-start | bytes 4030472 | tf_op jit(solution)/shard_map/ppermute | solution.py:492
  56.7 29.7 %collective-permute-start.3 = (bf16[8,656,128]{2,1,0:T(8,128)(2,1)S(1)}, bf16[8,656,128]{2,1,0:T(8,128)(2,1)S(1)}, u32[]{:S(2)}, u32[]{:S(2)}) collective-permute-start(bf16[8,656,128]{2,1,0:T(8,128)(2,1)S(1)} %pad_maximum_fusion), channel_id=1, source_target_pairs={{0,4},{1,5},{2,6},{3,7},{4,0},{5,1},{6,2},{7,3},{8,12},{9,13},{10,... | collective-permute-start | bytes 4030472 | tf_op jit(solution)/shard_map/ppermute | solution.py:492
  84.1 4.7 %copy-start.1 = (bf16[8,384]{1,0:T(8,128)(2,1)S(1)}, bf16[8,384]{1,0:T(8,128)(2,1)}, u32[]{:S(2)}) copy-start(bf16[8,384]{1,0:T(8,128)(2,1)} %param.6) | copy-start | bytes 18436
  84.1 5.9 %collective-permute-start.9 = (bf16[16,656,128]{2,1,0:T(8,128)(2,1)}, bf16[16,656,128]{2,1,0:T(8,128)(2,1)}, u32[]{:S(2)}, u32[]{:S(2)}) collective-permute-start(bf16[16,656,128]{2,1,0:T(8,128)(2,1)} %constant_dynamic-update-slice_fusion.5.half_a), channel_id=1, source_target_pairs={{0,1},{1,0},{2,3},{3,2},{4,5},{5,4},{6,7},{7,6},{8,9},{9,8},{10,11... | collective-permute-start | bytes 8060936 | tf_op jit(solution)/shard_map/ppermute | solution.py:492
  87.6 19.9 %collective-permute-start.4 = (bf16[16,656,128]{2,1,0:T(8,128)(2,1)}, bf16[16,656,128]{2,1,0:T(8,128)(2,1)}, u32[]{:S(2)}, u32[]{:S(2)}) collective-permute-start(bf16[16,656,128]{2,1,0:T(8,128)(2,1)} %constant_dynamic-update-slice_fusion.half_a), channel_id=1, source_target_pairs={{0,1},{1,0},{2,3},{3,2},{4,5},{5,4},{6,7},{7,6},{8,9},{9,8},{10,11... | collective-permute-start | bytes 8060936 | tf_op jit(solution)/shard_map/ppermute | solution.py:492
  146.9 128.0 %collective-permute-start.15 = (bf16[16,656,128]{2,1,0:T(8,128)(2,1)}, bf16[16,656,128]{2,1,0:T(8,128)(2,1)}, u32[]{:S(2)}, u32[]{:S(2)}) collective-permute-start(bf16[16,656,128]{2,1,0:T(8,128)(2,1)} %slice.86), channel_id=1, source_target_pairs={{0,1},{1,0},{2,3},{3,2},{4,5},{5,4},{6,7},{7,6},{8,9},{9,8},{10,11... | collective-permute-start | bytes 8060936 | tf_op jit(solution)/shard_map/ppermute | solution.py:492
  234.9 40.1 %copy-start = (bf16[32,656,128]{2,1,0:T(8,128)(2,1)S(1)}, bf16[32,656,128]{2,1,0:T(8,128)(2,1)}, u32[]{:S(2)}) copy-start(bf16[32,656,128]{2,1,0:T(8,128)(2,1)} %get-tuple-element.17) | copy-start | bytes 16121860
  234.9 92.6 %slice-start = ((s8[5373952]{0:T(1024)(128)(4,1)}), s8[4194304]{0:T(1024)(128)(4,1)S(1)}, s32[]{:S(2)}) async-start(s8[5373952]{0:T(1024)(128)(4,1)} %bitcast.6), calls=%async_computation | async-start | bytes 8388608
  237.0 90.5 %slice-start.1 = ((s8[5373952]{0:T(1024)(128)(4,1)}), s8[1179648]{0:T(1024)(128)(4,1)S(1)}, s32[]{:S(2)}) async-start(s8[5373952]{0:T(1024)(128)(4,1)} %bitcast.6), calls=%async_computation.1 | async-start | bytes 2359296
  237.0 90.5 %collective-permute-start.10 = (bf16[16,656,128]{2,1,0:T(8,128)(2,1)S(1)}, bf16[16,656,128]{2,1,0:T(8,128)(2,1)S(1)}, u32[]{:S(2)}, u32[]{:S(2)}) collective-permute-start(bf16[16,656,128]{2,1,0:T(8,128)(2,1)S(1)} %slice.76), channel_id=1, source_target_pairs={{0,1},{1,0},{2,3},{3,2},{4,5},{5,4},{6,7},{7,6},{8,9},{9,8},{10,11... | collective-permute-start | bytes 8060936 | tf_op jit(solution)/shard_map/ppermute | solution.py:492
  277.7 79.1 %collective-permute-start.16 = (bf16[8,656,128]{2,1,0:T(8,128)(2,1)S(1)}, bf16[8,656,128]{2,1,0:T(8,128)(2,1)S(1)}, u32[]{:S(2)}, u32[]{:S(2)}) collective-permute-start(bf16[8,656,128]{2,1,0:T(8,128)(2,1)S(1)} %slice.107), channel_id=1, source_target_pairs={{0,4},{1,5},{2,6},{3,7},{4,0},{5,1},{6,2},{7,3},{8,12},{9,13},{10,... | collective-permute-start | bytes 4030472 | tf_op jit(solution)/shard_map/ppermute | solution.py:492
  328.3 33.2 %collective-permute-start.11 = (bf16[8,656,128]{2,1,0:T(8,128)(2,1)S(1)}, bf16[8,656,128]{2,1,0:T(8,128)(2,1)S(1)}, u32[]{:S(2)}, u32[]{:S(2)}) collective-permute-start(bf16[8,656,128]{2,1,0:T(8,128)(2,1)S(1)} %slice.99), channel_id=1, source_target_pairs={{0,2},{1,3},{2,0},{3,1},{4,6},{5,7},{6,4},{7,5},{8,10},{9,11},{10,... | collective-permute-start | bytes 4030472 | tf_op jit(solution)/shard_map/ppermute | solution.py:492
  357.2 19.2 %collective-permute-start.17 = (bf16[4,656,128]{2,1,0:T(8,128)(2,1)S(1)}, bf16[4,656,128]{2,1,0:T(8,128)(2,1)S(1)}, u32[]{:S(2)}, u32[]{:S(2)}) collective-permute-start(bf16[4,656,128]{2,1,0:T(8,128)(2,1)S(1)} %slice.109), channel_id=1, source_target_pairs={{0,2},{1,3},{2,0},{3,1},{4,6},{5,7},{6,4},{7,5},{8,10},{9,11},{10,... | collective-permute-start | bytes 2015240 | tf_op jit(solution)/shard_map/ppermute | solution.py:492
  361.9 17.4 %copy-start.2 = (f32[16,384]{1,0:T(8,128)S(1)}, f32[16,384]{1,0:T(8,128)}, u32[]{:S(2)}) copy-start(f32[16,384]{1,0:T(8,128)} %get-tuple-element.15) | copy-start | bytes 73732
  361.9 17.4 %copy-start.3 = (f32[16,384]{1,0:T(8,128)S(1)}, f32[16,384]{1,0:T(8,128)}, u32[]{:S(2)}) copy-start(f32[16,384]{1,0:T(8,128)} %get-tuple-element.14) | copy-start | bytes 73732
  361.9 16.8 %collective-permute-start.12 = (bf16[4,656,128]{2,1,0:T(8,128)(2,1)S(1)}, bf16[4,656,128]{2,1,0:T(8,128)(2,1)S(1)}, u32[]{:S(2)}, u32[]{:S(2)}) collective-permute-start(bf16[4,656,128]{2,1,0:T(8,128)(2,1)S(1)} %slice.101), channel_id=1, source_target_pairs={{0,4},{1,5},{2,6},{3,7},{4,0},{5,1},{6,2},{7,3},{8,12},{9,13},{10,... | collective-permute-start | bytes 2015240 | tf_op jit(solution)/shard_map/ppermute | solution.py:492
  376.6 10.9 %collective-permute-start.18 = (bf16[2,656,128]{2,1,0:T(8,128)(2,1)S(1)}, bf16[2,656,128]{2,1,0:T(8,128)(2,1)S(1)}, u32[]{:S(2)}, u32[]{:S(2)}) collective-permute-start(bf16[2,656,128]{2,1,0:T(8,128)(2,1)S(1)} %slice.111), channel_id=1, source_target_pairs={{0,8},{1,9},{2,10},{3,11},{4,12},{5,13},{6,14},{7,15},{8,0},{9,1},... | collective-permute-start | bytes 1007624 | tf_op jit(solution)/shard_map/ppermute | solution.py:492
  378.9 17.6 %collective-permute-start.13 = (bf16[2,656,128]{2,1,0:T(8,128)(2,1)S(1)}, bf16[2,656,128]{2,1,0:T(8,128)(2,1)S(1)}, u32[]{:S(2)}, u32[]{:S(2)}) collective-permute-start(bf16[2,656,128]{2,1,0:T(8,128)(2,1)S(1)} %slice.103), channel_id=1, source_target_pairs={{0,8},{1,9},{2,10},{3,11},{4,12},{5,13},{6,14},{7,15},{8,0},{9,1},... | collective-permute-start | bytes 1007624 | tf_op jit(solution)/shard_map/ppermute | solution.py:492
  387.6 10.3 %collective-permute-start.19 = (bf16[1,656,128]{2,1,0:T(8,128)(2,1)S(1)}, bf16[1,656,128]{2,1,0:T(8,128)(2,1)S(1)}, u32[]{:S(2)}, u32[]{:S(2)}) collective-permute-start(bf16[1,656,128]{2,1,0:T(8,128)(2,1)S(1)} %slice.113), channel_id=1, source_target_pairs={{0,16},{1,17},{2,18},{3,19},{4,20},{5,21},{6,22},{7,23},{8,24},{9,... | collective-permute-start | bytes 503816 | tf_op jit(solution)/shard_map/ppermute | solution.py:492
  396.7 9.1 %collective-permute-start.14 = (bf16[1,656,128]{2,1,0:T(8,128)(2,1)S(1)}, bf16[1,656,128]{2,1,0:T(8,128)(2,1)S(1)}, u32[]{:S(2)}, u32[]{:S(2)}) collective-permute-start(bf16[1,656,128]{2,1,0:T(8,128)(2,1)S(1)} %slice.105), channel_id=1, source_target_pairs={{0,16},{1,17},{2,18},{3,19},{4,20},{5,21},{6,22},{7,23},{8,24},{9,... | collective-permute-start | bytes 503816 | tf_op jit(solution)/shard_map/ppermute | solution.py:492

commit v2 on v1

--- a/solution.py
+++ b/solution.py
@@ -50,7 +50,10 @@
     return lax.dot_general(a, b, (((0,), (0,)), ((), ())), preferred_element_type=F32)
 
 
-def slot_of(order, j):
+def slot_of(order, owner, me):
+    if order is None:
+        return owner
+    j = owner ^ me
     return sum(((j >> bit) & 1) << place for place, bit in enumerate(order))
 
 
@@ -76,8 +79,10 @@
 
 def load_weights(order, chunk, me, half_a, half_b, activ, stage, flat, sem, w):
     n = stage.shape[0]
-    first = pltpu.make_async_copy(half_a, stage.at[pl.ds(0, n // 2)], sem.at[0])
-    second = pltpu.make_async_copy(half_b, stage.at[pl.ds(n // 2, n // 2)], sem.at[1])
+    held = n // 2
+    source = half_b.at[pl.ds(half_b.shape[0] - held, held)]
+    first = pltpu.make_async_copy(half_a.at[pl.ds(0, held)], stage.at[pl.ds(0, held)], sem.at[0])
+    second = pltpu.make_async_copy(source, stage.at[pl.ds(held, held)], sem.at[1])
     first.start()
     second.start()
     first.wait()
@@ -85,7 +90,7 @@
     padded = stage.shape[1]
 
     def spread(owner, carry):
-        slot = slot_of(order, owner ^ me)
+        slot = slot_of(order[0], owner, me)
         flat[pl.ds(owner * chunk, padded), :] = stage[slot].astype(F32)
         return carry
 
@@ -145,12 +150,14 @@
     "slope": ((ROWS, MLP), BF16),
     "dpre": ((ROWS, MLP), BF16),
     "dbranch": ((ROWS, D), BF16),
+    "dbrancht": ((D, ROWS), BF16),
+    "n2t": ((D, ROWS), BF16),
     "dctx": ((ROWS, D), BF16),
     "dqkv": ((ROWS, 3 * D), BF16),
     "gqkv": ((D, 3 * D), F32),
     "go": ((D, D), F32),
     "g1": ((D, MLP), F32),
-    "g2": ((MLP, D), F32),
+    "g2": ((D, MLP), F32),
     "gbqkv": ((1, 3 * D), F32),
     "gbo": ((1, D), F32),
     "gb1": ((1, MLP), F32),
@@ -178,14 +185,14 @@
     s["n1"][...] = flat_rows(per_latent(normed_x) * (1.0 + scale_a) + shift_a).astype(BF16)
     s["qkvv"][...] = (mm(s["n1"][...], w["qkv"][...]) + w["bqkv"][...]).astype(BF16)
 
-    def attend(index, carry):
+    def attend(index):
         latent = index // (H // 2)
         pair = index % (H // 2)
-        rows = pl.ds(pl.multiple_of(latent * SEQ, SEQ), SEQ)
+        rows = pl.ds(latent * SEQ, SEQ)
         low_half = head_masks()
 
         def lanes(part):
-            return pl.ds(pl.multiple_of(part * D + pair * LANES, LANES), LANES)
+            return pl.ds(part * D + pair * LANES, LANES)
 
         q_heads = split_heads(s["qkvv"][rows, lanes(0)] * BF16(HD**-0.5), low_half)
         keys = s["qkvv"][rows, lanes(1)]
@@ -202,16 +209,16 @@
             both.append(probs)
         context = mm(jnp.concatenate(both, axis=1), jnp.concatenate(v_heads, axis=0))
         s["ctx"][rows, lanes(0)] = context.astype(BF16)
-        return carry
-
-    lax.fori_loop(0, PAIR * H // 2, attend, 0)
+
+    for index in range(PAIR * H // 2):
+        attend(index)
     attended = mm(s["ctx"][...], w["o"][...]) + w["bo"][...]
     middle = x + flat_rows(gate_a * per_latent(attended))
     normed_mid, inv_b = normalize(middle)
     s["n2"][...] = flat_rows(per_latent(normed_mid) * (1.0 + scale_b) + shift_b).astype(BF16)
 
-    def hidden(index, carry):
-        cols = pl.ds(pl.multiple_of(index * D, D), D)
+    def hidden(index):
+        cols = pl.ds(index * D, D)
         pre = mm(s["n2"][...], w["1"][:, cols]) + w["b1"][:, cols]
         square = pre * pre
         tanh = jnp.tanh(pre * (GELU_A + GELU_A * GELU_B * square))
@@ -221,9 +228,9 @@
             inner = GELU_A + 3.0 * GELU_A * GELU_B * square
             slope = half + 0.5 * pre * (1.0 - tanh * tanh) * inner
             s["slope"][:, cols] = slope.astype(BF16)
-        return carry
-
-    lax.fori_loop(0, MLP // D, hidden, 0)
+
+    for index in range(MLP // D):
+        hidden(index)
     branch = mm(s["act"][...], w["2"][...]) + w["b2"][...]
     result = middle + flat_rows(gate_b * per_latent(branch))
     return result, branch, attended, normed_x, inv_a, normed_mid, inv_b, mods
@@ -261,19 +268,21 @@
     put_mod(5, grad * branch)
     dbranch = flat_rows(gate_b * per_latent(grad)).astype(BF16)
     s["dbranch"][...] = dbranch
+    s["dbrancht"][...] = dbranch.T
+    s["n2t"][...] = s["n2"][...].T
     s["gb2"][...] += jnp.sum(dbranch.astype(F32), axis=0, keepdims=True)
 
-    def hidden(index, carry):
-        cols = pl.ds(pl.multiple_of(index * D, D), D)
-        s["g2"][cols, :] += mm_at(s["act"][:, cols], s["dbranch"][...])
+    def hidden(index):
+        cols = pl.ds(index * D, D)
+        s["g2"][:, cols] += mm(s["dbrancht"][...], s["act"][:, cols])
         dact = mm_bt(s["dbranch"][...], w["2"][cols, :])
         dpre = (dact * s["slope"][:, cols].astype(F32)).astype(BF16)
         s["dpre"][:, cols] = dpre
         s["gb1"][:, cols] += jnp.sum(dpre.astype(F32), axis=0, keepdims=True)
-        s["g1"][:, cols] += mm_at(s["n2"][...], dpre)
-        return carry
-
-    lax.fori_loop(0, MLP // D, hidden, 0)
+        s["g1"][:, cols] += mm(s["n2t"][...], dpre)
+
+    for index in range(MLP // D):
+        hidden(index)
     dnorm_b = mm_bt(s["dpre"][...], w["1"][...])
     put_mod(4, dnorm_b * normed_mid)
     put_mod(3, dnorm_b)
@@ -286,14 +295,14 @@
     s["go"][...] += mm_at(s["ctx"][...], dattended)
     s["dctx"][...] = mm_bt(dattended, w["o"][...]).astype(BF16)
 
-    def attend(index, carry):
+    def attend(index):
         latent = index // (H // 2)
         pair = index % (H // 2)
-        rows = pl.ds(pl.multiple_of(latent * SEQ, SEQ), SEQ)
+        rows = pl.ds(latent * SEQ, SEQ)
         low_half = head_masks()
 
         def lanes(part):
-            return pl.ds(pl.multiple_of(part * D + pair * LANES, LANES), LANES)
+            return pl.ds(part * D + pair * LANES, LANES)
 
         q_heads = split_heads(s["qkvv"][rows, lanes(0)] * BF16(HD**-0.5), low_half)
         k_heads = split_heads(s["qkvv"][rows, lanes(1)] * BF16(HD**-0.5), low_half)
@@ -309,16 +318,17 @@
             probs = s["probs"][index * 2 + head].astype(F32)
             dscores.append((probs * (dprobs - row_dot)).astype(BF16))
         dquery = mm(jnp.concatenate(dscores, axis=1), jnp.concatenate(k_heads, axis=0))
-        dkey = mm_at(dscores[0], q_heads[0]) + mm_at(dscores[1], q_heads[1])
-        dvalue = mm_at(s["probs"][index * 2], dctx_heads[0]) + mm_at(
-            s["probs"][index * 2 + 1], dctx_heads[1]
-        )
+        qt = jnp.concatenate([q_heads[0].T, q_heads[1].T], axis=1)
+        dt = jnp.concatenate([dctx_heads[0].T, dctx_heads[1].T], axis=1)
+        both = jnp.concatenate([s["probs"][index * 2], s["probs"][index * 2 + 1]], axis=0)
+        dkey = mm(qt, jnp.concatenate(dscores, axis=0)).T
+        dvalue = mm(dt, both).T
         s["dqkv"][rows, lanes(0)] = dquery.astype(BF16)
         s["dqkv"][rows, lanes(1)] = dkey.astype(BF16)
         s["dqkv"][rows, lanes(2)] = dvalue.astype(BF16)
-        return carry
-
-    lax.fori_loop(0, PAIR * H // 2, attend, 0)
+
+    for index in range(PAIR * H // 2):
+        attend(index)
     dqkv = s["dqkv"][...]
     s["gqkv"][...] += mm_at(s["n1"][...], dqkv)
     s["gbqkv"][...] += jnp.sum(dqkv.astype(F32), axis=0, keepdims=True)
@@ -358,12 +368,12 @@
     vector(s["gbo"], R_BO, D)
     matrix(of_ref(s["g1"]), R_1, D, MLP)
     vector(s["gb1"], R_B1, MLP)
-    matrix(of_ref(s["g2"]), R_2, MLP, D)
+    matrix(lambda c: s["g2"][c * LANES : (c + 1) * LANES, :].T, R_2, MLP, D)
     vector(s["gb2"], R_B2, D)
     flat[R_END : flat.shape[0], :] = jnp.zeros((flat.shape[0] - R_END, LANES), F32)
 
     def gather(owner, carry):
-        slot = slot_of(order, owner ^ me)
+        slot = slot_of(order[1], owner, me)
         stage[slot] = flat[pl.ds(owner * chunk, padded), :].astype(BF16)
         return carry
 
@@ -422,7 +432,7 @@
 
 
 def run_forward(order, chunk, scalars, halves, activ, x):
-    n, padded = 2 * halves[0].shape[0], halves[0].shape[1]
+    n, padded = lax.axis_size("dev"), halves[0].shape[1]
     names, shapes = scratch_of([WEIGHT_SCRATCH, ACT_SCRATCH])
     block = pl.BlockSpec((PAIR, SEQ, D), lambda i, sc: (i, 0, 0))
     whole = pl.BlockSpec((16, D), lambda i, sc: (0, 0))
@@ -451,7 +461,7 @@
 
 
 def run_backward(order, chunk, scalars, halves, activ, x, grad, last):
-    n, padded = 2 * halves[0].shape[0], halves[0].shape[1]
+    n, padded = lax.axis_size("dev"), halves[0].shape[1]
     names, shapes = scratch_of([WEIGHT_SCRATCH, ACT_SCRATCH, BACK_SCRATCH])
     block = pl.BlockSpec((PAIR, SEQ, D), lambda i, sc: (i, 0, 0))
     whole = pl.BlockSpec((16, D), lambda i, sc: (0, 0))
@@ -492,48 +502,80 @@
     return lax.ppermute(values, "dev", [(i, i ^ (1 << bit)) for i in range(n)])
 
 
-def gather_halves(order, n, shard):
+def add_low(kept, sent):
+    return (kept.astype(F32) + sent.astype(F32)).astype(BF16)
+
+
+def gather_halves(n, shard):
+    bits = n.bit_length() - 1
     held = shard
-    for bit in order[:-1]:
+    for bit in range(bits - 1, 2, -1):
         held = jnp.concatenate([held, swap(held, bit, n)], axis=0)
-    return held, swap(held, order[-1], n)
-
-
-def scatter_sum(order, n, parts):
-    for bit in order[::-1]:
-        half = parts.shape[0] // 2
-        sent = swap(parts[half:], bit, n)
-        total = parts[:half].astype(F32) + sent.astype(F32)
-        parts = total.astype(BF16) if half > 1 else total
-    return parts
+    rows = held.shape[1] // 2
+    left, right = held[:, :rows], held[:, rows:]
+    left = jnp.stack([left, swap(left, 2, n)], axis=0)
+    right = jnp.stack([right, swap(right, 1, n)], axis=0)
+    left = jnp.stack([left, swap(left, 1, n)], axis=0)
+    right = jnp.stack([right, swap(right, 2, n)], axis=1)
+    held = jnp.concatenate([left, right], axis=3).reshape((n // 2, 2 * rows, LANES))
+    return held, swap(held, 0, n)
+
+
+def halve(parts, bit, n):
+    half = parts.shape[0] // 2
+    return add_low(parts[:half], swap(parts[half:], bit, n))
+
+
+def scatter_rest(order, n, parts, sent):
+    parts = add_low(parts[: parts.shape[0] // 2], sent)
+    for bit in order[-2::-1]:
+        parts = halve(parts, bit, n)
+    return parts.astype(F32)
+
+
+def scatter_sum_split(n, parts):
+    bits = n.bit_length() - 1
+    parts = halve(parts, 0, n)
+    rows = parts.shape[1] // 2
+    parts = parts.reshape((2, 2, n // 8) + parts.shape[1:])
+    left, right = parts[:, :, :, :rows], parts[:, :, :, rows:]
+    left = add_low(left[0], swap(left[1], 1, n))
+    right = add_low(right[:, 0], swap(right[:, 1], 2, n))
+    left = add_low(left[0], swap(left[1], 2, n))
+    right = add_low(right[0], swap(right[1], 1, n))
+    parts = jnp.concatenate([left, right], axis=1)
+    for bit in range(3, bits):
+        parts = halve(parts, bit, n)
+    return parts.astype(F32)
 
 
 def shards(latents, cond, params, cotangent, counts):
     n = lax.axis_size("dev")
     chunk = params.shape[1] // LANES
-    padded = (chunk + 15) // 16 * 16
+    padded = (chunk + 31) // 32 * 32
     bits = n.bit_length() - 1
-    first = list(range(bits - 1, -1, -1))
-    second = list(first)
-    if bits > 2:
-        second[-2], second[-3] = second[-3], second[-2]
-    orders = [tuple(first), tuple(second)]
+    first = tuple(range(bits - 1, -1, -1))
+    second = first[:-3] + (2, 0, 1)
     scalars = jnp.stack([counts[0], lax.axis_index("dev").astype(jnp.int32)])
     cond_float = cond.astype(F32)
     activ = jax.nn.silu(cond_float).astype(BF16)
     activ = jnp.pad(activ, ((0, 16 - activ.shape[0]), (0, 0)))
     rows = params.reshape(LAYERS, chunk, LANES)
     rows = jnp.pad(rows, ((0, 0), (0, padded - chunk), (0, 0)))
-    weights = [gather_halves(orders[i], n, rows[i : i + 1]) for i in range(LAYERS)]
-    middle = run_forward(orders[0], chunk, scalars, weights[0], activ, latents)
+    gathered = lax.all_gather(rows[1], "dev", axis=0)
+    weights_2 = (gathered, gathered)
+    weights_1 = gather_halves(n, rows[:1])
+    middle = run_forward((first, first), chunk, scalars, weights_1, activ, latents)
     output, grad_mid, dactiv_2, parts_2 = run_backward(
-        orders[1], chunk, scalars, weights[1], activ, middle, cotangent, True
+        (None, second), chunk, scalars, weights_2, activ, middle, cotangent, True
     )
-    sum_2 = scatter_sum(orders[1], n, parts_2)
+    sent_2 = swap(parts_2[n // 2 :], second[-1], n)
     grad_in, dactiv_1, parts_1 = run_backward(
-        orders[0], chunk, scalars, weights[0], activ, latents, grad_mid, False
+        (first, first), chunk, scalars, weights_1, activ, latents, grad_mid, False
     )
-    sum_1 = scatter_sum(orders[0], n, parts_1)
+    parts_1, sent_2 = lax.optimization_barrier((parts_1, sent_2))
+    sum_2 = scatter_rest(second, n, parts_2, sent_2)
+    sum_1 = scatter_sum_split(n, parts_1)
     param_grads = jnp.concatenate([sum_1, sum_2], axis=0)[:, :chunk].reshape(LAYERS, chunk * LANES)
     _, silu_pull = jax.vjp(jax.nn.silu, cond_float)
     cond_grad = silu_pull((dactiv_1 + dactiv_2)[: cond.shape[0]])[0]

time: 407 us -> 353 us (0.87)
  starting transfers between devices: 168 us -> 104 us
  waiting for transfers between devices: 125 us -> 87.1 us
  Pallas kernels: 88.9 us -> 124 us
  between operations: 1.55 us -> 15.2 us
  local copies, waits for them, and re-layouts: 17.2 us -> 11.9 us
    ppermute x20 -> x19, starting transfers between devices: 168 us -> 104 us  [swap(): return lax.ppermute(values, 'dev', [(i, i ^ 1 << bit) for i in range(n)])]
    ppermute x20 -> x19, waiting for transfers between devices: 125 us -> 87.1 us  [swap(): return lax.ppermute(values, 'dev', [(i, i ^ 1 << bit) for i in range(n)])]
    pallas_call x2, Pallas kernels: 71.4 us -> 102 us  [run_backward(): pl.pallas_call(functools.partial(backward_kernel, order, chunk, names, la...]
    pallas_call x1, Pallas kernels: 17.5 us -> 21.8 us  [run_forward(): pl.pallas_call(functools.partial(forward_kernel, order, chunk, names), gr...]
  transfers between devices with their start and end apart: 20 -> 20, of which waited for: 13 -> 13; matrix products, arithmetic and copies ran while one was open for 4% -> 2% of each run, Pallas kernels for 13% -> 19%
where the time goes in v2:
time: 353 us; the launch traced here: 349 us
  Pallas kernels  124 us (35%)
  starting transfers between devices  104 us (29%)
  waiting for transfers between devices  87.1 us (25%)
  between operations  15.2 us (4%)
  local copies, waits for them, and re-layouts  11.9 us (3%)
  other arithmetic  7.29 us (2%)
    ppermute x19, starting transfers between devices, swap(): return lax.ppermute(values, 'dev', [(i, i ^ 1 << bit) for i in range(n)])  104 us
    pallas_call x2, Pallas kernels, run_backward(): pl.pallas_call(functools.partial(backward_kernel, order, chunk, names, la...  102 us
    ppermute x19, waiting for transfers between devices, swap(): return lax.ppermute(values, 'dev', [(i, i ^ 1 << bit) for i in range(n)])  87.1 us
    pallas_call x1, Pallas kernels, run_forward(): pl.pallas_call(functools.partial(forward_kernel, order, chunk, names), gr...  21.8 us
  transfers between devices with their start and end apart: 20, of which 13 were waited for; matrix products, arithmetic and copies ran while one was open for 2% of the time, Pallas kernels for 19%

profile of v2, /device:TPU:0, one launch (start us, length us, event | category | flops | bytes accessed | tf_op | source)
XLA Modules:
  0.0 349.3 jit_solution(999882842386406105)
XLA Ops:
  7.2 0.0 all-gather.2.cloned.1.call-start
  7.2 1.5 reshape.31
  8.8 0.7 pad_slice_fusion.2
  9.4 0.0 all-gather.2.cloned.1.call-update
  9.5 4.1 %collective-permute-start = (bf16[1,672,128]{2,1,0:T(8,128)(2,1)S(1)}, bf16[1,672,128]{2,1,0:T(8,128)(2,1)S(1)}, u32[]{:S(2)}, u32[]{:S(2)}) collective-permute-start(bf16[1,672,128]{2,1,0:T(8,128)(2,1)S(1)} %get-tuple-element.32), channel_id=1, source_target_pairs={{0,16},{1,17},{2,18},{3,19},{4,20},{5,21},{6,22},{7,23},{8,24},{9,... | collective-permute-start | bytes 516104 | tf_op jit(solution)/shard_map/ppermute | solution.py:502
  13.6 8.1 %collective-permute-done = bf16[1,672,128]{2,1,0:T(8,128)(2,1)S(1)} collective-permute-done((bf16[1,672,128]{2,1,0:T(8,128)(2,1)S(1)}, bf16[1,672,128]{2,1,0:T(8,128)(2,1)S(1)}, u32[]{:S(2)}, u32[]{:S(2)}) %collective-permute-start) | collective-permute-done | bytes 172064 | tf_op jit(solution)/shard_map/ppermute | solution.py:502
  21.7 0.8 collective-permute-start.1
  22.5 11.4 %collective-permute-done.1 = bf16[2,672,128]{2,1,0:T(8,128)(2,1)S(1)} collective-permute-done((bf16[2,672,128]{2,1,0:T(8,128)(2,1)S(1)}, bf16[2,672,128]{2,1,0:T(8,128)(2,1)S(1)}, u32[]{:S(2)}, u32[]{:S(2)}) %collective-permute-start.1) | collective-permute-done | bytes 344096 | tf_op jit(solution)/shard_map/ppermute | solution.py:502
  33.8 0.1 pad_maximum_fusion
  33.9 0.2 slice_bitcast_fusion.9
  34.1 1.3 collective-permute-start.2
  35.4 1.8 collective-permute-start.4
  37.1 5.1 %collective-permute-done.2 = bf16[4,336,128]{2,1,0:T(8,128)(2,1)S(1)} collective-permute-done((bf16[4,336,128]{2,1,0:T(8,128)(2,1)S(1)}, bf16[4,336,128]{2,1,0:T(8,128)(2,1)S(1)}, u32[]{:S(2)}, u32[]{:S(2)}) %collective-permute-start.2) | collective-permute-done | bytes 344096 | tf_op jit(solution)/shard_map/ppermute | solution.py:502
  42.2 0.1 fusion.12
  42.3 1.5 collective-permute-start.3
  43.8 1.9 collective-permute-done.4
  45.7 0.1 fusion.11
  45.8 0.1 collective-permute-start.5
  45.9 17.1 %collective-permute-done.3 = bf16[2,4,336,128]{3,2,1,0:T(8,128)(2,1)S(1)} collective-permute-done((bf16[2,4,336,128]{3,2,1,0:T(8,128)(2,1)S(1)}, bf16[2,4,336,128]{3,2,1,0:T(8,128)(2,1)S(1)}, u32[]{:S(2)}, u32[]{:S(2)}) %collective-permute-start.3) | collective-permute-done | bytes 688160 | tf_op jit(solution)/shard_map/ppermute | solution.py:502
  62.9 0.2 maximum_maximum_fusion
  63.2 0.0 copy-start.1
  63.2 0.2 copy.18
  63.4 1.5 copy-done
  65.5 0.6 pad.9.activ
  66.1 0.6 pad_add_fusion.scalars
  66.7 3.5 %collective-permute-done.6.half_b = bf16[16,672,128]{2,1,0:T(8,128)(2,1)} collective-permute-done((bf16[16,672,128]{2,1,0:T(8,128)(2,1)S(1)}, bf16[16,672,128]{2,1,0:T(8,128)(2,1)}, u32[]{:S(2)}, u32[]{:S(2)}) %collective-permute-start.6) | collective-permute-done | bytes 2752544 | tf_op jit(solution)/shard_map/ppermute | solution.py:502
  70.2 21.8 %block_forward.1.x_ref = f32[8,256,384]{2,1,0:T(8,128)} custom-call(s32[2]{0:T(128)} %pad_add_fusion.scalars, bf16[16,672,128]{2,1,0:T(8,128)(2,1)} %bitcast.60, bf16[16,672,128]{2,1,0:T(8,128)(2,1)} %collective-permute-done.6.half_b, bf16[16,384]{1,0:T(8,128)(2,1)} %pad.9.activ, bf16[8,256,384]{2,1,0:T(8,128)(2,1)} %x_ref.3), custom_call_target="tpu_custom_call" | custom-call | flops 8000000000 | bytes 20000000 | tf_op jit(solution)/shard_map/block_forward/pallas_call | solution.py:440
  92.0 0.0 all-gather.2.cloned.1.call-done.half_a.half_b
  92.1 57.1 %block_backward.2 = (bf16[8,256,384]{2,1,0:T(8,128)(2,1)}, f32[8,256,384]{2,1,0:T(8,128)}, f32[16,384]{1,0:T(8,128)}, bf16[32,672,128]{2,1,0:T(8,128)(2,1)}) custom-call(s32[2]{0:T(128)} %pad_add_fusion.scalars, bf16[32,672,128]{2,1,0:T(8,128)(2,1)} %all-gather.2.cloned.1.call-done.half_a.half_b, ...), custom_call_target="tpu_custom_call" | custom-call | flops 32000000000 | bytes 40000000 | tf_op jit(solution)/shard_map/block_backward/pallas_call | solution.py:478
  149.2 3.6 %slice.102 = bf16[16,672,128]{2,1,0:T(8,128)(2,1)} slice(bf16[32,672,128]{2,1,0:T(8,128)(2,1)} %get-tuple-element.19), slice={[16:32], [0:672], [0:128]} | slice | bytes 5505024 | tf_op jit(solution)/shard_map/slice | solution.py:572
  152.8 40.9 %collective-permute-start.7 = (bf16[16,672,128]{2,1,0:T(8,128)(2,1)}, bf16[16,672,128]{2,1,0:T(8,128)(2,1)}, u32[]{:S(2)}, u32[]{:S(2)}) collective-permute-start(bf16[16,672,128]{2,1,0:T(8,128)(2,1)} %slice.102), channel_id=1, source_target_pairs={{0,2},{1,3},{2,0},{3,1},{4,6},{5,7},{6,4},{7,5},{8,10},{9,11},{10,... | collective-permute-start | bytes 8257544 | tf_op jit(solution)/shard_map/ppermute | solution.py:502
  193.7 45.0 %block_backward.3 = (f32[8,256,384]{2,1,0:T(8,128)}, f32[16,384]{1,0:T(8,128)}, bf16[32,672,128]{2,1,0:T(8,128)(2,1)}) custom-call(s32[2]{0:T(128)} %pad_add_fusion.scalars, bf16[16,672,128]{2,1,0:T(8,128)(2,1)} %bitcast.61, bf16[16,672,128]{2,1,0:T(8,128)(2,1)} %collective-permute-done.6.half_b, bf16[16,384]{1,0:T(8,128)(2,1)} %pad.9.activ, ...), custom_call_target="tpu_custom_call" | custom-call | flops 32000000000 | bytes 40000000 | tf_op jit(solution)/shard_map/block_backward/pallas_call | solution.py:478
  238.7 2.1 slice.104
  240.8 0.1 collective-permute-start.8
  240.9 3.4 add_convert_fusion
  244.3 0.1 slice.144
  244.4 0.5 collective-permute-start.15
  244.9 1.1 collective-permute-done.8
  246.0 0.7 add_convert_fusion.1
  246.8 27.6 %collective-permute-start.11 = (bf16[2,4,336,128]{3,2,1,0:T(8,128)(2,1)S(1)}, bf16[2,4,336,128]{3,2,1,0:T(8,128)(2,1)S(1)}, u32[]{:S(2)}, u32[]{:S(2)}) collective-permute-start(bf16[2,4,336,128]{3,2,1,0:T(8,128)(2,1)S(1)} %slice_bitcast_fusion), channel_id=1, source_target_pairs={{0,4},{1,5},{2,6},{3,7},{4,0},{5,1},{6,2},{7,3},{8,12},{9,13},{10,... | collective-permute-start | bytes 2064392 | tf_op jit(solution)/shard_map/ppermute | solution.py:502
  274.4 1.6 collective-permute-start.9
  276.0 0.4 add_convert_fusion.2
  276.5 1.3 collective-permute-start.16
  277.8 12.9 %collective-permute-done.11 = bf16[2,4,336,128]{3,2,1,0:T(8,128)(2,1)S(1)} collective-permute-done((bf16[2,4,336,128]{3,2,1,0:T(8,128)(2,1)S(1)}, bf16[2,4,336,128]{3,2,1,0:T(8,128)(2,1)S(1)}, u32[]{:S(2)}, u32[]{:S(2)}) %collective-permute-start.11) | collective-permute-done | bytes 688160 | tf_op jit(solution)/shard_map/ppermute | solution.py:502
  290.7 1.1 collective-permute-done.9
  291.8 0.4 fusion.1
  292.2 1.0 collective-permute-start.10
  293.2 0.0 copy-start.2
  293.3 1.8 collective-permute-start.12
  295.1 10.3 %collective-permute-done.16 = bf16[4,672,128]{2,1,0:T(8,128)(2,1)S(1)} collective-permute-done((bf16[4,672,128]{2,1,0:T(8,128)(2,1)S(1)}, bf16[4,672,128]{2,1,0:T(8,128)(2,1)S(1)}, u32[]{:S(2)}, u32[]{:S(2)}) %collective-permute-start.16) | collective-permute-done | bytes 688160 | tf_op jit(solution)/shard_map/ppermute | solution.py:502
  305.4 0.2 add_convert_fusion.3
  305.6 2.5 collective-permute-start.17
  308.2 4.3 %collective-permute-done.10 = bf16[4,336,128]{2,1,0:T(8,128)(2,1)S(1)} collective-permute-done((bf16[4,336,128]{2,1,0:T(8,128)(2,1)S(1)}, bf16[4,336,128]{2,1,0:T(8,128)(2,1)S(1)}, u32[]{:S(2)}, u32[]{:S(2)}) %collective-permute-start.10) | collective-permute-done | bytes 344096 | tf_op jit(solution)/shard_map/ppermute | solution.py:502
  312.5 0.1 fusion.3
  312.6 0.1 fusion.2
  312.7 2.5 collective-permute-start.13
  315.2 0.6 fusion.10
  315.9 0.1 add_convert_fusion.4
  316.0 7.5 %collective-permute-start.18 = (bf16[1,672,128]{2,1,0:T(8,128)(2,1)S(1)}, bf16[1,672,128]{2,1,0:T(8,128)(2,1)S(1)}, u32[]{:S(2)}, u32[]{:S(2)}) collective-permute-start(bf16[1,672,128]{2,1,0:T(8,128)(2,1)S(1)} %slice.150), channel_id=1, source_target_pairs={{0,16},{1,17},{2,18},{3,19},{4,20},{5,21},{6,22},{7,23},{8,24},{9,... | collective-permute-start | bytes 516104 | tf_op jit(solution)/shard_map/ppermute | solution.py:502
  323.5 1.8 collective-permute-done.13
  325.4 0.1 add_convert_fusion.5
  325.5 7.0 %collective-permute-start.14 = (bf16[1,672,128]{2,1,0:T(8,128)(2,1)S(1)}, bf16[1,672,128]{2,1,0:T(8,128)(2,1)S(1)}, u32[]{:S(2)}, u32[]{:S(2)}) collective-permute-start(bf16[1,672,128]{2,1,0:T(8,128)(2,1)S(1)} %slice.142), channel_id=1, source_target_pairs={{0,16},{1,17},{2,18},{3,19},{4,20},{5,21},{6,22},{7,23},{8,24},{9,... | collective-permute-start | bytes 516104 | tf_op jit(solution)/shard_map/ppermute | solution.py:502
  332.5 8.4 %collective-permute-done.14 = bf16[1,672,128]{2,1,0:T(8,128)(2,1)S(1)} collective-permute-done((bf16[1,672,128]{2,1,0:T(8,128)(2,1)S(1)}, bf16[1,672,128]{2,1,0:T(8,128)(2,1)S(1)}, u32[]{:S(2)}, u32[]{:S(2)}) %collective-permute-start.14) | collective-permute-done | bytes 172064 | tf_op jit(solution)/shard_map/ppermute | solution.py:502
  341.0 1.2 copy.25
  (31 shorter events, 0.5 us)
Async XLA Ops:
  7.2 84.9 %all-gather.2.cloned.1.call-start = ((), (), s32[]{:S(2)}) async-start(), calls=%async_computation | async-start | bytes 5677056 | tf_op jit(solution)/shard_map/all_gather | solution.py:565
  9.5 12.2 %collective-permute-start = (bf16[1,672,128]{2,1,0:T(8,128)(2,1)S(1)}, bf16[1,672,128]{2,1,0:T(8,128)(2,1)S(1)}, u32[]{:S(2)}, u32[]{:S(2)}) collective-permute-start(bf16[1,672,128]{2,1,0:T(8,128)(2,1)S(1)} %get-tuple-element.32), channel_id=1, source_target_pairs={{0,16},{1,17},{2,18},{3,19},{4,20},{5,21},{6,22},{7,23},{8,24},{9,... | collective-permute-start | bytes 516104 | tf_op jit(solution)/shard_map/ppermute | solution.py:502
  21.7 12.2 %collective-permute-start.1 = (bf16[2,672,128]{2,1,0:T(8,128)(2,1)S(1)}, bf16[2,672,128]{2,1,0:T(8,128)(2,1)S(1)}, u32[]{:S(2)}, u32[]{:S(2)}) collective-permute-start(bf16[2,672,128]{2,1,0:T(8,128)(2,1)S(1)} %pad_maximum_fusion.4), channel_id=1, source_target_pairs={{0,8},{1,9},{2,10},{3,11},{4,12},{5,13},{6,14},{7,15},{8,0},{9,1},... | collective-permute-start | bytes 1032200 | tf_op jit(solution)/shard_map/ppermute | solution.py:502
  34.1 8.1 %collective-permute-start.2 = (bf16[4,336,128]{2,1,0:T(8,128)(2,1)S(1)}, bf16[4,336,128]{2,1,0:T(8,128)(2,1)S(1)}, u32[]{:S(2)}, u32[]{:S(2)}) collective-permute-start(bf16[4,336,128]{2,1,0:T(8,128)(2,1)S(1)} %get-tuple-element.29), channel_id=1, source_target_pairs={{0,4},{1,5},{2,6},{3,7},{4,0},{5,1},{6,2},{7,3},{8,12},{9,13},{10,... | collective-permute-start | bytes 1032200 | tf_op jit(solution)/shard_map/ppermute | solution.py:502
  35.4 10.4 %collective-permute-start.4 = (bf16[4,336,128]{2,1,0:T(8,128)(2,1)S(1)}, bf16[4,336,128]{2,1,0:T(8,128)(2,1)S(1)}, u32[]{:S(2)}, u32[]{:S(2)}) collective-permute-start(bf16[4,336,128]{2,1,0:T(8,128)(2,1)S(1)} %get-tuple-element.28), channel_id=1, source_target_pairs={{0,2},{1,3},{2,0},{3,1},{4,6},{5,7},{6,4},{7,5},{8,10},{9,11},{10,... | collective-permute-start | bytes 1032200 | tf_op jit(solution)/shard_map/ppermute | solution.py:502
  42.3 20.6 %collective-permute-start.3 = (bf16[2,4,336,128]{3,2,1,0:T(8,128)(2,1)S(1)}, bf16[2,4,336,128]{3,2,1,0:T(8,128)(2,1)S(1)}, u32[]{:S(2)}, u32[]{:S(2)}) collective-permute-start(bf16[2,4,336,128]{3,2,1,0:T(8,128)(2,1)S(1)} %get-tuple-element.25), channel_id=1, source_target_pairs={{0,2},{1,3},{2,0},{3,1},{4,6},{5,7},{6,4},{7,5},{8,10},{9,11},{10,... | collective-permute-start | bytes 2064392 | tf_op jit(solution)/shard_map/ppermute | solution.py:502
  45.8 17.1 %collective-permute-start.5 = (bf16[2,4,336,128]{3,2,1,0:T(8,128)(2,1)S(1)}, bf16[2,4,336,128]{3,2,1,0:T(8,128)(2,1)S(1)}, u32[]{:S(2)}, u32[]{:S(2)}) collective-permute-start(bf16[2,4,336,128]{3,2,1,0:T(8,128)(2,1)S(1)} %get-tuple-element.31), channel_id=1, source_target_pairs={{0,4},{1,5},{2,6},{3,7},{4,0},{5,1},{6,2},{7,3},{8,12},{9,13},{10,... | collective-permute-start | bytes 2064392 | tf_op jit(solution)/shard_map/ppermute | solution.py:502
  63.2 2.4 copy-start.1
  63.4 1.5 copy-start
  64.9 5.4 %collective-permute-start.6 = (bf16[16,672,128]{2,1,0:T(8,128)(2,1)S(1)}, bf16[16,672,128]{2,1,0:T(8,128)(2,1)}, u32[]{:S(2)}, u32[]{:S(2)}) collective-permute-start(bf16[16,672,128]{2,1,0:T(8,128)(2,1)S(1)} %bitcast.59), channel_id=1, source_target_pairs={{0,1},{1,0},{2,3},{3,2},{4,5},{5,4},{6,7},{7,6},{8,9},{9,8},{10,11... | collective-permute-start | bytes 8257544 | tf_op jit(solution)/shard_map/ppermute | solution.py:502
  152.8 85.9 %collective-permute-start.7 = (bf16[16,672,128]{2,1,0:T(8,128)(2,1)}, bf16[16,672,128]{2,1,0:T(8,128)(2,1)}, u32[]{:S(2)}, u32[]{:S(2)}) collective-permute-start(bf16[16,672,128]{2,1,0:T(8,128)(2,1)} %slice.102), channel_id=1, source_target_pairs={{0,2},{1,3},{2,0},{3,1},{4,6},{5,7},{6,4},{7,5},{8,10},{9,11},{10,... | collective-permute-start | bytes 8257544 | tf_op jit(solution)/shard_map/ppermute | solution.py:502
  238.7 7.3 %slice-start = ((s8[5505024]{0:T(1024)(128)(4,1)}), s8[4194304]{0:T(1024)(128)(4,1)S(1)}, s32[]{:S(2)}) async-start(s8[5505024]{0:T(1024)(128)(4,1)} %bitcast.57), calls=%async_computation.1 | async-start | bytes 8388608
  240.8 5.2 %slice-start.1 = ((s8[5505024]{0:T(1024)(128)(4,1)}), s8[1310720]{0:T(1024)(128)(4,1)S(1)}, s32[]{:S(2)}) async-start(s8[5505024]{0:T(1024)(128)(4,1)} %bitcast.57), calls=%async_computation.2 | async-start | bytes 2621440
  240.8 5.2 %collective-permute-start.8 = (bf16[16,672,128]{2,1,0:T(8,128)(2,1)S(1)}, bf16[16,672,128]{2,1,0:T(8,128)(2,1)S(1)}, u32[]{:S(2)}, u32[]{:S(2)}) collective-permute-start(bf16[16,672,128]{2,1,0:T(8,128)(2,1)S(1)} %slice.104), channel_id=1, source_target_pairs={{0,1},{1,0},{2,3},{3,2},{4,5},{5,4},{6,7},{7,6},{8,9},{9,8},{10,11... | collective-permute-start | bytes 8257544 | tf_op jit(solution)/shard_map/ppermute | solution.py:502
  244.4 31.6 %collective-permute-start.15 = (bf16[8,672,128]{2,1,0:T(8,128)(2,1)S(1)}, bf16[8,672,128]{2,1,0:T(8,128)(2,1)S(1)}, u32[]{:S(2)}, u32[]{:S(2)}) collective-permute-start(bf16[8,672,128]{2,1,0:T(8,128)(2,1)S(1)} %slice.144), channel_id=1, source_target_pairs={{0,1},{1,0},{2,3},{3,2},{4,5},{5,4},{6,7},{7,6},{8,9},{9,8},{10,11... | collective-permute-start | bytes 4128776 | tf_op jit(solution)/shard_map/ppermute | solution.py:502
  246.8 43.9 %collective-permute-start.11 = (bf16[2,4,336,128]{3,2,1,0:T(8,128)(2,1)S(1)}, bf16[2,4,336,128]{3,2,1,0:T(8,128)(2,1)S(1)}, u32[]{:S(2)}, u32[]{:S(2)}) collective-permute-start(bf16[2,4,336,128]{3,2,1,0:T(8,128)(2,1)S(1)} %slice_bitcast_fusion), channel_id=1, source_target_pairs={{0,4},{1,5},{2,6},{3,7},{4,0},{5,1},{6,2},{7,3},{8,12},{9,13},{10,... | collective-permute-start | bytes 2064392 | tf_op jit(solution)/shard_map/ppermute | solution.py:502
  274.4 17.4 %collective-permute-start.9 = (bf16[2,4,336,128]{3,2,1,0:T(8,128)(2,1)S(1)}, bf16[2,4,336,128]{3,2,1,0:T(8,128)(2,1)S(1)}, u32[]{:S(2)}, u32[]{:S(2)}) collective-permute-start(bf16[2,4,336,128]{3,2,1,0:T(8,128)(2,1)S(1)} %slice_bitcast_fusion.2), channel_id=1, source_target_pairs={{0,2},{1,3},{2,0},{3,1},{4,6},{5,7},{6,4},{7,5},{8,10},{9,11},{10,... | collective-permute-start | bytes 2064392 | tf_op jit(solution)/shard_map/ppermute | solution.py:502
  276.5 29.0 %collective-permute-start.16 = (bf16[4,672,128]{2,1,0:T(8,128)(2,1)S(1)}, bf16[4,672,128]{2,1,0:T(8,128)(2,1)S(1)}, u32[]{:S(2)}, u32[]{:S(2)}) collective-permute-start(bf16[4,672,128]{2,1,0:T(8,128)(2,1)S(1)} %slice.146), channel_id=1, source_target_pairs={{0,4},{1,5},{2,6},{3,7},{4,0},{5,1},{6,2},{7,3},{8,12},{9,13},{10,... | collective-permute-start | bytes 2064392 | tf_op jit(solution)/shard_map/ppermute | solution.py:502
  292.2 20.2 %collective-permute-start.10 = (bf16[4,336,128]{2,1,0:T(8,128)(2,1)S(1)}, bf16[4,336,128]{2,1,0:T(8,128)(2,1)S(1)}, u32[]{:S(2)}, u32[]{:S(2)}) collective-permute-start(bf16[4,336,128]{2,1,0:T(8,128)(2,1)S(1)} %slice_bitcast_fusion.6), channel_id=1, source_target_pairs={{0,4},{1,5},{2,6},{3,7},{4,0},{5,1},{6,2},{7,3},{8,12},{9,13},{10,... | collective-permute-start | bytes 1032200 | tf_op jit(solution)/shard_map/ppermute | solution.py:502
  293.2 22.0 %copy-start.2 = (f32[16,384]{1,0:T(8,128)S(1)}, f32[16,384]{1,0:T(8,128)}, u32[]{:S(2)}) copy-start(f32[16,384]{1,0:T(8,128)} %get-tuple-element.17) | copy-start | bytes 73732
  293.2 22.0 %copy-start.3 = (f32[16,384]{1,0:T(8,128)S(1)}, f32[16,384]{1,0:T(8,128)}, u32[]{:S(2)}) copy-start(f32[16,384]{1,0:T(8,128)} %get-tuple-element.16) | copy-start | bytes 73732
  293.3 19.3 %collective-permute-start.12 = (bf16[4,336,128]{2,1,0:T(8,128)(2,1)S(1)}, bf16[4,336,128]{2,1,0:T(8,128)(2,1)S(1)}, u32[]{:S(2)}, u32[]{:S(2)}) collective-permute-start(bf16[4,336,128]{2,1,0:T(8,128)(2,1)S(1)} %slice_bitcast_fusion.4), channel_id=1, source_target_pairs={{0,2},{1,3},{2,0},{3,1},{4,6},{5,7},{6,4},{7,5},{8,10},{9,11},{10,... | collective-permute-start | bytes 1032200 | tf_op jit(solution)/shard_map/ppermute | solution.py:502
  305.6 10.2 %collective-permute-start.17 = (bf16[2,672,128]{2,1,0:T(8,128)(2,1)S(1)}, bf16[2,672,128]{2,1,0:T(8,128)(2,1)S(1)}, u32[]{:S(2)}, u32[]{:S(2)}) collective-permute-start(bf16[2,672,128]{2,1,0:T(8,128)(2,1)S(1)} %slice.148), channel_id=1, source_target_pairs={{0,8},{1,9},{2,10},{3,11},{4,12},{5,13},{6,14},{7,15},{8,0},{9,1},... | collective-permute-start | bytes 1032200 | tf_op jit(solution)/shard_map/ppermute | solution.py:502
  312.7 12.6 %collective-permute-start.13 = (bf16[2,672,128]{2,1,0:T(8,128)(2,1)S(1)}, bf16[2,672,128]{2,1,0:T(8,128)(2,1)S(1)}, u32[]{:S(2)}, u32[]{:S(2)}) collective-permute-start(bf16[2,672,128]{2,1,0:T(8,128)(2,1)S(1)} %pad_maximum_fusion.3), channel_id=1, source_target_pairs={{0,8},{1,9},{2,10},{3,11},{4,12},{5,13},{6,14},{7,15},{8,0},{9,1},... | collective-permute-start | bytes 1032200 | tf_op jit(solution)/shard_map/ppermute | solution.py:502
  316.0 16.5 %collective-permute-start.18 = (bf16[1,672,128]{2,1,0:T(8,128)(2,1)S(1)}, bf16[1,672,128]{2,1,0:T(8,128)(2,1)S(1)}, u32[]{:S(2)}, u32[]{:S(2)}) collective-permute-start(bf16[1,672,128]{2,1,0:T(8,128)(2,1)S(1)} %slice.150), channel_id=1, source_target_pairs={{0,16},{1,17},{2,18},{3,19},{4,20},{5,21},{6,22},{7,23},{8,24},{9,... | collective-permute-start | bytes 516104 | tf_op jit(solution)/shard_map/ppermute | solution.py:502
  325.5 15.4 %collective-permute-start.14 = (bf16[1,672,128]{2,1,0:T(8,128)(2,1)S(1)}, bf16[1,672,128]{2,1,0:T(8,128)(2,1)S(1)}, u32[]{:S(2)}, u32[]{:S(2)}) collective-permute-start(bf16[1,672,128]{2,1,0:T(8,128)(2,1)S(1)} %slice.142), channel_id=1, source_target_pairs={{0,16},{1,17},{2,18},{3,19},{4,20},{5,21},{6,22},{7,23},{8,24},{9,... | collective-permute-start | bytes 516104 | tf_op jit(solution)/shard_map/ppermute | solution.py:502
Sparse Core Ops, SparseCore 0:
  11.5 74.1 all-gather.1
